TPU v7x, 32 devices: a whole 2x2x4 slice. The times are simulated.
32 devices in a mesh: tower: 2 (over core), batch: 16 (over z, y, x).
Axes of the slice: x: 2, y: 2, z: 4, core: 2. Of those that a mesh axis runs over, the one named last changes fastest.
Arguments:
- root_state: bfloat16 [4096, 256], P('batch', 'tower'), may hold values from -6 to 6
- cond_table: bfloat16 [36, 256], replicated, may hold values from -6 to 6
- block_gain: bfloat16 [2, 3, 256], P('tower'), may hold values from 0.25 to 1.75
- w_in: bfloat16 [2, 3, 256, 256], P('tower'), may hold values from -0.375 to 0.375
- w_out: bfloat16 [2, 3, 256, 256], P('tower'), may hold values from -0.375 to 0.375
- value_head: bfloat16 [2, 256, 601], P('tower'), may hold values from -0.75 to 0.75
- reward_head: bfloat16 [256, 601], replicated, may hold values from -0.75 to 0.75
- small_head: bfloat16 [256, 36], replicated, may hold values from -0.75 to 0.75
- unroll_len: int32 [4096], P('batch'), may hold values from 5 to 10, as said below
- actions: int32 [10, 4096], P(None, 'batch'), may hold values from 0 to 3
- codes: int32 [10, 4096], P(None, 'batch'), may hold values from 0 to 31
- policy_target: int32 [10, 4096], P(None, 'batch'), may hold values from 0 to 3
- value_bins: int32 [2, 10, 4096], P(None, None, 'batch'), may hold values from 0 to 600
- reward_bins: int32 [10, 4096], P(None, 'batch'), may hold values from 0 to 600
Outputs:
- latents: bfloat16 [2, 10, 4096, 256], P('tower', None, 'batch')
- value_logits: bfloat16 [2, 10, 4096, 601], P('tower', None, 'batch')
- row_loss: float32 [4096], P('batch')
- layer_rms: float32 [2, 10, 3, 2], P('tower')
- grad_root: float32 [4096, 256], P('batch', 'tower')
- grad_cond: float32 [36, 256], replicated
- grad_gain: float32 [2, 3, 256], P('tower')
- grad_w_in: float32 [2, 3, 256, 256], P('tower')
- grad_w_out: float32 [2, 3, 256, 256], P('tower')
- grad_value_head: float32 [2, 256, 601], P('tower')
- grad_reward_head: float32 [256, 601], replicated
- grad_small_head: float32 [256, 36], replicated
Inputs may be any that keep to these rules, and one draw needn't show every extreme that they name: `unroll_len`: each position unrolls either 10 or 5 steps.
All inputs are finite; a program needn't handle non-finite values.
Results may differ from a plain program's by a relative error of at most 0.013.
Values may be sent and summed in bfloat16 or wider, within the bound.
No kernel may reach another device: no remote copies, remote signals or barrier semaphores. Data moves between devices by JAX's collectives and lax.ppermute only.
A program may use at most 64 MiB of HBM per device.

v0:
```python
import functools

import jax
import jax.numpy as jnp
from jax import lax
from jax.experimental import pallas as pl
from jax.experimental.pallas import tpu as pltpu
from jax.sharding import PartitionSpec as P

ACTIONS = 4
LANES = 128
MIB = 1024 * 1024
FORWARD_LIMIT = 20 * MIB
BACKWARD_LIMIT = 20 * MIB
SMALL_LIMIT = 12 * MIB
epsilon = 1e-06
very_negative = -1e30
F32 = jnp.float32
BF16 = jnp.bfloat16


def natural(left, right):
    return lax.dot_general(left, right, (((1,), (0,)), ((), ())), preferred_element_type=F32)


def by_rows(left, right):
    return lax.dot_general(left, right, (((0,), (0,)), ((), ())), preferred_element_type=F32)


def by_lanes(left, right):
    return lax.dot_general(left, right, (((1,), (1,)), ((), ())), preferred_element_type=F32)


def round_up(value, unit):
    return (value + unit - 1) // unit * unit


def lane_sum(value):
    return jnp.sum(value, axis=-1, keepdims=True)


def inverse_rms(hidden):
    return lax.rsqrt(lane_sum(hidden * hidden) * (1.0 / hidden.shape[-1]) + epsilon)


def weave(*tasks):
    tasks = [(list(task)) for task in tasks]
    longest = max(len(task) for task in tasks)
    done = [0] * len(tasks)
    for turn in range(longest):
        for which, task in enumerate(tasks):
            until = (turn + 1) * len(task) // longest
            while done[which] < until:
                task[done[which]]()
                done[which] += 1


def cuts(length, unit=160):
    return [(start, min(start + unit, length)) for start in range(0, length, unit)]


class Sizes:
    def __init__(self, steps, rows, blocks, width, bins, table_rows, parts):
        self.steps, self.rows, self.blocks, self.width = steps, rows, blocks, width
        self.bins, self.table_rows, self.parts = bins, table_rows, parts
        self.calls = 2 * blocks
        self.pair = 2 if steps % 2 == 0 else 1
        self.wide = round_up(bins, 32)
        self.held = round_up(table_rows, 16)
        self.stack = (self.wide + self.held, 2 * self.wide + self.held)
        self.depth = tuple(round_up(rows_in, LANES) for rows_in in self.stack)
        half = self.wide // 2
        self.value_at = self.calls * width
        self.sums_at = self.value_at + self.wide
        self.kinds = 2 * self.calls
        self.gain_row = self.kinds + 1
        self.reward_at = self.sums_at + round_up(self.gain_row + blocks, 16)
        self.small_at = self.reward_at + half
        self.cond_at = self.small_at + self.held
        self.shared_end = self.cond_at + self.held
        self.total = round_up(self.shared_end, 16 * parts)
        self.head_rows = self.cond_at - self.value_at


def forward_kernel(
    sizes, tower_ref,
    root_hbm, lengths_hbm, actions_hbm, codes_hbm, policy_hbm, value_bins_hbm, reward_bins_hbm,
    table_hbm, gains_hbm, in_hbm, out_hbm, value_hbm, reward_hbm, small_hbm,
    root_any, in_got, out_got, value_any, gains_got,
    lat, lat_own, lat_away, entry, after, slope, side, dlat, dlast, loss, head_grads, turned, code_rows, gains,
    root_own, root_got, lengths, actions, codes, policy, value_bins, reward_bins,
    table_in, gains_own, value_own, value_got, reward_in, small_in, sems,
    state, past0, past1, table, weights, heads0, heads1, acc0, acc1,
    logits0, logits1, cot0, cot1, sums, squares,
):
    s = sizes
    pair = s.pair
    turn = pl.program_id(0)
    first_step = turn * pair
    tower_id = tower_ref[0]
    rows, width, wide = s.rows, s.width, s.wide

    @pl.when(turn == 0)
    def _():
        here = pl.ds(pl.multiple_of(tower_id * rows, rows), rows)

        def matrices(kind, tower):
            return weights.at[pl.ds(kind * s.calls + tower * s.blocks, s.blocks)]

        moves = [
            (in_hbm, matrices(0, tower_id)),
            (out_hbm, matrices(1, tower_id)),
            (in_got, matrices(0, 1 - tower_id)),
            (out_got, matrices(1, 1 - tower_id)),
            (value_hbm, value_own),
            (value_any, value_got),
            (reward_hbm, reward_in),
            (small_hbm, small_in),
            (table_hbm, table_in),
            (gains_hbm, gains_own),
            (root_hbm.at[here], root_own),
            (root_any.at[here], root_got),
            (actions_hbm.at[:, here], actions),
            (codes_hbm.at[:, here], codes),
            (lengths_hbm.at[:, here], lengths),
            (policy_hbm.at[:, here], policy),
            (value_bins_hbm.at[:, :, here], value_bins),
            (reward_bins_hbm.at[:, here], reward_bins),
        ]
        moves = [
            pltpu.make_async_copy(source, target, sems.at[place])
            for place, (source, target) in enumerate(moves)
        ]
        for move in moves:
            move.start()
        for target in (
            gains, table, heads0, heads1, past0, past1, cot0, cot1, acc0, acc1, sums, squares, loss
        ):
            target[...] = jnp.zeros_like(target)
        for move in moves:
            move.wait()
        first = tower_id == 0
        code_rows[0] = actions[...]
        code_rows[1] = codes[...] + ACTIONS
        state[:, 0 : width // 2] = jnp.where(first, root_own[...], root_got[...])
        state[:, width // 2 : width] = jnp.where(first, root_got[...], root_own[...])
        gains[tower_id, 0 : s.blocks, :] = gains_own[...].astype(F32)
        gains[1 - tower_id, 0 : s.blocks, :] = gains_got[...].astype(F32)
        table[0 : s.table_rows, :] = table_in[...]
        heads0[0 : s.bins, :] = jnp.where(first, value_own[...], value_got[...])
        heads1[0 : s.bins, :] = jnp.where(first, value_got[...], value_own[...])
        heads1[wide : wide + s.bins, :] = reward_in[...]
        heads0[wide : wide + s.table_rows, :] = small_in[...]
        heads1[2 * wide : 2 * wide + s.table_rows, :] = small_in[...]

    eights = lax.broadcasted_iota(jnp.int32, (8, pair * rows), 0)
    before = jnp.maximum(first_step - pair, 0)

    def pair_row(kind, at_step, lead=()):
        return jnp.concatenate(
            [kind[(pl.ds(at_step + offset, 1),) + lead] for offset in range(pair)], axis=1
        )

    def live_rows(at_step):
        return jnp.concatenate(
            [(at_step + offset < lengths[...]).astype(F32) for offset in range(pair)], axis=1
        )

    kinds = []
    for offset in range(pair):
        step = first_step + offset
        kinds.append((step < lengths[...]).astype(F32))
        kinds.append(actions[pl.ds(step, 1), :].astype(F32))
        kinds.append((codes[pl.ds(step, 1), :] + ACTIONS).astype(F32))
    kinds.append(jnp.zeros((8 - len(kinds), rows), F32))
    columns = jnp.concatenate(kinds, axis=0).T

    def heads(tower, live_row, at_step, put):
        latent = past0 if tower == 0 else past1
        stack, logits, cot, acc = (
            (heads0, logits0, cot0, acc0) if tower == 0 else (heads1, logits1, cot1, acc1)
        )
        pick = lambda kind: pair_row(kind, at_step)
        value_goal = pair_row(value_bins, at_step, (tower,))
        spans = [(0, wide, 0, s.bins, value_goal)]
        if tower == 1:
            spans.append((wide, wide, 0, s.bins, pick(reward_bins)))
            spans.append((2 * wide, s.held, 0, ACTIONS, pick(policy)))
        else:
            spans.append((wide, s.held, ACTIONS, s.table_rows, pick(codes) + ACTIONS))

        def make_logits(start, stop):
            logits[start:stop, :] = by_lanes(stack[start:stop, :], latent[...])

        def eight_rows(value):
            return value.reshape(-1, 8, pair * rows)

        def mask(at, length, first, last):
            for start in range(0, length, 8):
                if start < first or start + 8 > last:
                    inside = (eights >= first - start) & (eights < last - start)
                    place = slice(at + start, at + start + 8)
                    logits[place, :] = jnp.where(inside, logits[place, :], very_negative)

        def find_top(at, start, stop, kept):
            top = jnp.max(eight_rows(logits[at + start : at + stop, :]), axis=0)
            kept["top"] = jnp.maximum(kept["top"], top) if "top" in kept else top

        def end_top(kept):
            kept["top"] = jnp.max(kept["top"], axis=0, keepdims=True)

        def make_terms(at, start, stop, goal, kept):
            place = slice(at + start, at + stop)
            value = logits[place, :]
            spot = lax.broadcasted_iota(jnp.int32, value.shape, 0)
            term = jnp.exp(value - kept["top"])
            logits[place, :] = term
            hit = spot == goal - start
            total = jnp.sum(eight_rows(term), axis=0)
            picked = jnp.sum(eight_rows(jnp.where(hit, value, 0.0)), axis=0)
            kept["total"] = kept["total"] + total if "total" in kept else total
            kept["picked"] = kept["picked"] + picked if "picked" in kept else picked

        def end_terms(kept):
            total = jnp.sum(kept["total"], axis=0, keepdims=True)
            picked = jnp.sum(kept["picked"], axis=0, keepdims=True)
            kept["scale"] = live_row / total
            row_loss = live_row * (jnp.log(total) + kept["top"] - picked)
            for offset in range(pair):
                loss[0:1, :] += row_loss[:, offset * rows : (offset + 1) * rows]

        def make_cotangent(at, start, stop, goal, kept):
            place = slice(at + start, at + stop)
            term = logits[place, :]
            spot = lax.broadcasted_iota(jnp.int32, term.shape, 0)
            hit = spot == goal - start
            cot[place, :] = (term * kept["scale"] - jnp.where(hit, live_row, 0.0)).astype(BF16)

        def make_grads(start, stop):
            acc[start:stop, :] += natural(cot[start:stop, :], latent[...])

        def make_latent():
            d_latent = by_rows(cot[...], stack[...])
            for offset in range(pair):
                put[offset, tower] = d_latent[offset * rows : (offset + 1) * rows]

        large = cuts(acc.shape[0], 320)
        pieces = [functools.partial(make_logits, *cut) for cut in large]
        for at, length, first, last, goal in spans:
            kept = {}
            each = cuts(length)
            pieces.append(functools.partial(mask, at, length, first, last))
            pieces += [functools.partial(find_top, at, *cut, kept) for cut in each]
            pieces.append(functools.partial(end_top, kept))
            pieces += [functools.partial(make_terms, at, *cut, goal, kept) for cut in each]
            pieces.append(functools.partial(end_terms, kept))
            pieces += [functools.partial(make_cotangent, at, *cut, goal, kept) for cut in each]
        return pieces + [make_latent] + [functools.partial(make_grads, *cut) for cut in large]

    def columns_of(offset, tower):
        live = columns[:, 3 * offset : 3 * offset + 1]
        return live, columns[:, 3 * offset + 1 + tower : 3 * offset + 2 + tower]

    def embedding(offset, tower):
        _, code = columns_of(offset, tower)
        spot = lax.broadcasted_iota(jnp.int32, (rows, table.shape[0]), 1)
        onehot = jnp.where(spot.astype(F32) == code, 1.0, 0.0).astype(BF16)
        return natural(onehot, table[...])

    def tower_call(offset, tower, chain):
        live, _ = columns_of(offset, tower)

        def scale_rows():
            row_squares = lane_sum(chain["hidden"] * chain["hidden"])
            return row_squares, lax.rsqrt(row_squares * (1.0 / width) + epsilon)

        def keep_squares(block, row_squares):
            place = 2 * (tower * s.blocks + block)
            total = jnp.sum(live * row_squares, axis=0, keepdims=True) * (1.0 / LANES)
            squares[offset, place : place + 1, 0:LANES] = jnp.broadcast_to(total, (1, LANES))

        def end_block(block):
            branch = chain["product"]
            chain["hidden"] = chain["hidden"] + branch
            return branch

        def keep_branch(block, branch):
            spot = 2 * (tower * s.blocks + block) + 1
            squares[offset, spot : spot + 1, :] = jnp.sum(
                branch * branch * live, axis=0, keepdims=True
            )

        def into(block):
            place = tower * s.blocks + block
            if block > 0:
                branch = end_block(block - 1)
            gained = chain["hidden"] * gains[tower, block : block + 1, :]
            chain["product"] = natural(gained.astype(BF16), weights[place])
            row_squares, inv_scale = scale_rows()
            chain["scale"] = inv_scale
            entry[offset, place] = (gained * inv_scale).astype(BF16)
            side[offset, place] = jnp.broadcast_to(inv_scale, (rows, LANES))
            if block > 0:
                keep_squares(block - 1, row_squares)
                keep_branch(block - 1, branch)

        def out_of(block):
            place = tower * s.blocks + block
            u = chain["product"] * chain["scale"]
            gate = 0.5 * jnp.tanh(0.5 * u) + 0.5
            after_rows = (u * gate).astype(BF16)
            chain["product"] = natural(after_rows, weights[s.calls + place])
            after[offset, place] = after_rows
            slope[offset, place] = gate * (1.0 + u * (1.0 - gate))

        def finish():
            branch = end_block(s.blocks - 1)
            row_squares, inv_scale = scale_rows()
            latent = (chain["hidden"] * inv_scale).astype(BF16)
            chain[offset, tower] = latent
            following = (offset, 1) if tower == 0 else (offset + 1, 0)
            if following in chain:
                chain["hidden"] = latent.astype(F32) + chain[following]

            def keep():
                side[offset, s.calls + tower] = jnp.broadcast_to(inv_scale, (rows, LANES))
                lat[offset, tower] = latent
                keep_squares(s.blocks - 1, row_squares)
                keep_branch(s.blocks - 1, branch)
                if tower == 0:
                    total = jnp.sum(live, axis=0, keepdims=True) * (1.0 / LANES)
                    squares[offset, s.kinds : s.kinds + 1, 0:LANES] = jnp.broadcast_to(
                        total, (1, LANES)
                    )

            return keep

        pieces = []
        for block in range(s.blocks):
            pieces += [functools.partial(into, block), functools.partial(out_of, block)]
        return pieces, finish

    chain = {
        (offset, tower): embedding(offset, tower) for offset in range(pair) for tower in range(2)
    }
    chain["hidden"] = state[...].astype(F32) + chain[0, 0]
    pieces = []
    keeps = []

    def begin_next(finish, into):
        keeps.append(finish())
        into()
        keeps.pop()()

    ending = None
    for offset in range(pair):
        for tower in range(2):
            calls, finish = tower_call(offset, tower, chain)
            if ending is not None:
                calls[0] = functools.partial(begin_next, ending, calls[0])
            pieces += calls
            ending = finish
    pieces.append(lambda: ending()())

    turns = -(-2 * s.calls // (s.steps // pair))

    def turn_weights(which):
        matrix = jnp.minimum(turn * turns + which, 2 * s.calls - 1)
        turned[matrix] = weights[matrix].T

    live_before = jnp.where(turn > 0, live_rows(before), 0.0)
    weave(
        pieces,
        heads(1, live_before, before, dlat)
        + heads(0, live_before, before, dlat)
        + [functools.partial(turn_weights, which) for which in range(turns)],
    )
    first = tower_id == 0
    at_lane = lax.broadcasted_iota(jnp.int32, sums.shape, 1)
    for offset in range(pair):
        at = slice(offset * rows, (offset + 1) * rows)
        after_state, next_state = chain[offset, 0], chain[offset, 1]
        past0[at, :] = after_state
        past1[at, :] = next_state
        lat_own[offset] = jnp.where(first, after_state, next_state)
        lat_away[offset] = jnp.where(first, next_state, after_state)
        if offset == pair - 1:
            state[...] = next_state
        total = lane_sum(squares[offset])
        sums[...] = jnp.where(at_lane == first_step + offset, total, sums[...])

    @pl.when(turn == pl.num_programs(0) - 1)
    def _():
        live_now = live_rows(first_step)
        weave(heads(1, live_now, first_step, dlast), heads(0, live_now, first_step, dlast))
        half = wide // 2
        head_grads[...] = jnp.zeros_like(head_grads)
        head_grads[0, 0:wide, :] = acc0[0:wide, :].astype(BF16)
        head_grads[1, 0:wide, :] = acc1[0:wide, :].astype(BF16)
        small = acc0[wide : wide + s.held, :] + acc1[2 * wide : 2 * wide + s.held, :]
        at = s.small_at - s.value_at
        head_grads[0, at : at + s.held, :] = small.astype(BF16)
        for tower in range(2):
            put = s.reward_at - s.value_at
            at = wide + tower * half
            head_grads[tower, put : put + half, :] = acc1[at : at + half, :].astype(BF16)
            head_grads[tower, wide : wide + sums.shape[0], 0:LANES] = sums[...].astype(BF16)


def backward_kernel(
    sizes, tower_ref,
    lat, entry, after, slope, side, dlat, dlast, code_rows, gains_in, turned, head_grads,
    own, away, root_own, root_away,
    carry, gain_sum, cond_sum, grads, gains, inverse_gains, d_after_kept, d_before_kept,
    d_hidden_kept,
):
    s = sizes
    pair = s.pair
    turn = pl.program_id(0)
    first_step = s.steps - pair * (turn + 1)
    tower_id = tower_ref[0]
    blocks, width = s.blocks, s.width

    @pl.when(turn == 0)
    def _():
        gains[...] = jnp.ones_like(gains)
        gains[:, 0:blocks, :] = gains_in[:, 0:blocks, :]
        inverse_gains[...] = 1.0 / gains[...]
        carry[...] = jnp.zeros_like(carry)
        grads[...] = jnp.zeros_like(grads)
        gain_sum[...] = jnp.zeros_like(gain_sum)
        cond_sum[...] = jnp.zeros_like(cond_sum)

    def over_lanes(column):
        return jnp.concatenate([column] * (width // LANES), axis=1)

    def stacked(parts):
        return jnp.concatenate(parts, axis=0)

    def add_grads(matrix, rows_of, place, kept, now):
        later = [kept[offset, place] for offset in range(1, pair)]
        grads[matrix // s.calls, matrix % s.calls] += by_rows(
            stacked([rows_of[offset, place] for offset in range(pair)]), stacked([now] + later)
        )

    def add_cond(offset, tower, d_hidden):
        if offset > 0:
            d_hidden_kept[offset, tower] = d_hidden.astype(BF16)
            return
        code = jnp.concatenate(
            [code_rows[tower, pl.ds(first_step + step, 1), :] for step in range(pair)], axis=1
        )
        spots = lax.broadcasted_iota(jnp.int32, (cond_sum.shape[0], pair * s.rows), 0)
        onehot = jnp.where(spots == code, 1.0, 0.0).astype(BF16)
        parts = [d_hidden.astype(BF16)]
        parts += [d_hidden_kept[step, tower] for step in range(1, pair)]
        cond_sum[...] += natural(onehot, stacked(parts))

    behind = []

    def catch_up():
        while behind:
            behind.pop(0)()

    def tower_back(offset, tower, d_latent):
        normed = lat[offset, tower]
        normed_wide = normed.astype(F32)
        inv_scale = over_lanes(side[offset, s.calls + tower])
        base = inv_scale * d_latent
        slant = inv_scale * (lane_sum(d_latent * normed_wide) * (1.0 / width))
        for block in reversed(range(blocks)):
            place = tower * blocks + block
            matrix = tower * s.calls + block
            both = natural(
                jnp.concatenate([normed, base.astype(BF16)], axis=0), turned[s.calls + place]
            )
            d_hidden = base - slant * normed_wide
            d_branch = d_hidden.astype(BF16)
            entry_wide = entry[offset, place].astype(F32)
            inv_scale = over_lanes(side[offset, place])
            catch_up()
            d_after = both[s.rows :] - slant * both[: s.rows]
            d_before = (d_after * slope[offset, place]).astype(BF16)
            d_entry = natural(d_before, turned[place])
            if offset > 0:
                d_after_kept[offset, place] = d_branch
                d_before_kept[offset, place] = d_before
            else:
                add_grads(matrix + blocks, after, place, d_after_kept, d_branch)
                behind.append(
                    functools.partial(add_grads, matrix, entry, place, d_before_kept, d_before)
                )
            gain = gains[tower, block : block + 1, :]
            normed_wide = entry_wide * inverse_gains[tower, block : block + 1, :]
            normed = normed_wide.astype(BF16)
            product = d_entry * entry_wide
            base = d_hidden + inv_scale * (d_entry * gain)
            slant = inv_scale * (lane_sum(product) * (1.0 / width))

            def add_gain(tower=tower, block=block, product=product):
                gain_sum[tower, block : block + 1, :] += jnp.sum(product, axis=0, keepdims=True)

            behind.append(add_gain)
        d_hidden = base - slant * normed_wide
        behind.append(functools.partial(add_cond, offset, tower, d_hidden))
        return d_hidden

    def from_heads(offset, tower):
        return jnp.where(turn == 0, dlast[offset, tower], dlat[offset, tower])

    d_state = carry[...]
    for offset in reversed(range(pair)):
        for tower in (1, 0):
            d_state = tower_back(offset, tower, d_state + from_heads(offset, tower))
    catch_up()
    carry[...] = d_state

    @pl.when(turn == pl.num_programs(0) - 1)
    def _():
        left = d_state[:, 0 : width // 2].astype(BF16)
        right = d_state[:, width // 2 : width].astype(BF16)
        root_own[...] = jnp.where(tower_id == 0, left, right)
        root_away[...] = jnp.where(tower_id == 0, right, left)
        gain_sum[...] = gain_sum[...] * inverse_gains[...]
        lines = lax.broadcasted_iota(jnp.int32, (s.reward_at - s.sums_at, width), 0)
        for target, which in ((own, tower_id), (away, 1 - tower_id)):
            for matrix in range(s.calls):
                at = matrix * width
                target[at : at + width, :] = grads[which, matrix].astype(BF16)
            target[s.value_at : s.cond_at, :] = head_grads[which]
            sums = head_grads[which, s.wide : s.wide + lines.shape[0], :].astype(F32)
            for block in range(blocks):
                gain = gain_sum[which, block : block + 1, :]
                sums = jnp.where(lines == s.gain_row + block, gain, sums)
            target[s.sums_at : s.reward_at, :] = sums.astype(BF16)
            here = jnp.where(which == 0, cond_sum[...], 0.0)
            target[s.cond_at : s.shared_end, :] = here.astype(BF16)
            if s.total > s.shared_end:
                target[s.shared_end :, :] = jnp.zeros((s.total - s.shared_end, width), BF16)


def logits_kernel(sizes, tower_ref, lat_own, lat_got, value_own, latents, logits):
    rows = sizes.rows
    tower_id = tower_ref[0]
    at_own = pl.ds(pl.multiple_of(tower_id * rows, rows), rows)
    at_got = pl.ds(pl.multiple_of((1 - tower_id) * rows, rows), rows)
    for offset in range(sizes.pair):
        latents[offset, at_own, :] = lat_own[offset]
        latents[offset, at_got, :] = lat_got[offset]
        logits[offset] = by_lanes(value_own[...], latents[offset]).astype(BF16)


def add_and_split_kernel(count, digit_ref, *refs):
    inputs, outputs = refs[:count], refs[count:]
    digit = digit_ref[0]
    for other, target in enumerate(outputs):
        part = digit ^ other
        total = inputs[0][part].astype(F32)
        for source in inputs[1:]:
            total = total + source[part].astype(F32)
        target[...] = total.astype(BF16)


def unpack_own_kernel(sizes, scalars, *refs):
    s = sizes
    factor = len(refs) - 7
    digit, tower_id = scalars[0], scalars[1]
    w_in, w_out, value, gain, rms, flat, held = refs[factor:]
    width = s.width
    length = refs[0].shape[0]
    for other, source in enumerate(refs[:factor]):
        at = pl.multiple_of((digit ^ other) * length, 16)
        flat[pl.ds(at, length), :] = source[...]
    for block in range(s.blocks):
        at = block * width
        w_in[block] = flat[at : at + width, :].astype(F32)
        at = (s.blocks + block) * width
        w_out[block] = flat[at : at + width, :].astype(F32)
    value[:, 0, :] = flat[s.value_at : s.sums_at, :].astype(F32)[0 : s.bins]
    sums = flat[s.sums_at : s.reward_at, :].astype(F32)
    for block in range(s.blocks):
        gain[block] = sums[s.gain_row + block : s.gain_row + block + 1, :]
    held[...] = sums[:, 0:LANES]
    count = jnp.maximum(held[s.kinds : s.kinds + 1, 0 : s.steps], 1.0)
    for block in range(s.blocks):
        for kind in range(2):
            spot = tower_id * s.calls + 2 * block + kind
            square = held[pl.ds(spot, 1), 0 : s.steps]
            rms[block, kind : kind + 1, :] = jnp.sqrt(jnp.maximum(square, 0.0) / (count * width))


def unpack_shared_kernel(sizes, tower_ref, mine, got, reward, small, cond, joined):
    s = sizes
    tower_id = tower_ref[0]
    half = s.wide // 2
    joined[pl.ds(pl.multiple_of(tower_id * half, 8), half), :] = mine[0:half, :].astype(F32)
    joined[pl.ds(pl.multiple_of((1 - tower_id) * half, 8), half), :] = got[0:half, :].astype(F32)
    reward[...] = joined[0 : s.bins, :]
    for target, at in ((small, s.small_at), (cond, s.cond_at)):
        rows = slice(at - s.reward_at, at - s.reward_at + s.held)
        target[...] = (mine[rows, :].astype(F32) + got[rows, :].astype(F32))[0 : s.table_rows]


def whole(shape):
    return pl.BlockSpec(shape, lambda step, tower: (0,) * len(shape))


def swap(value, axis, mask):
    pairs = [(source, source ^ mask) for source in range(lax.axis_size(axis))]
    return lax.ppermute(value, axis, pairs)


AXES = ("tower", "batch")


def exchange_rounds(batch_size):
    factors, left = [], batch_size
    while left > 1:
        factors.append(4 if left % 4 == 0 else 2)
        left //= factors[-1]
    rounds, stride = [], 1
    for factor in factors:
        rounds.append((factor, stride))
        stride *= factor
    turned = rounds[::-1] if len(set(factors)) == 1 else rounds
    return [(one[0], (one[1], two[1])) for one, two in zip(rounds, turned)]


def swap_within(value, strides, other, batch_size):
    pairs = [
        (tower * batch_size + index, tower * batch_size + (index ^ (other * strides[tower])))
        for tower in range(2)
        for index in range(batch_size)
    ]
    return lax.ppermute(value, AXES, pairs)


def my_digit(factor, strides):
    stride = jnp.where(lax.axis_index("tower") == 0, strides[0], strides[1])
    return (lax.axis_index("batch") // stride) % factor


def add_kernel(*refs):
    total = refs[0][...].astype(F32)
    for source in refs[1:-1]:
        total = total + source[...].astype(F32)
    refs[-1][...] = total.astype(BF16)


def add_up(parts):
    return pl.pallas_call(
        add_kernel,
        out_shape=jax.ShapeDtypeStruct(parts[0].shape, BF16),
        compiler_params=pltpu.CompilerParams(vmem_limit_bytes=SMALL_LIMIT),
        name="add_up",
    )(*parts)


def exchange(value, rounds, batch_size, beside, given, last_kernel):
    factor, strides = rounds[0]
    digit = my_digit(factor, strides)
    rows, width = value[0].shape
    rows = rows // factor
    split = pl.pallas_call(
        functools.partial(add_and_split_kernel, len(value)),
        grid_spec=pltpu.PrefetchScalarGridSpec(
            num_scalar_prefetch=1,
            grid=(1,),
            in_specs=[whole((factor, rows, width))] * len(value),
            out_specs=[whole((rows, width))] * factor,
        ),
        out_shape=[pltpu.HBM((rows, width), BF16)] * factor,
        compiler_params=pltpu.CompilerParams(vmem_limit_bytes=SMALL_LIMIT),
        name="add_and_split",
    )(digit[None], *[part.reshape(factor, rows, width) for part in value])
    split, given = lax.optimization_barrier((split, given))
    held = [split[0]] + [
        swap_within(split[other], strides, other, batch_size) for other in range(1, factor)
    ]
    done = beside(given)
    held, done = lax.optimization_barrier((held, done))
    for size, steps in rounds[1:]:
        bit = 1
        while bit < size:
            block = add_up(held)
            held = [block, swap_within(block, steps, bit, batch_size)]
            bit *= 2
    block = add_up(held)
    held = [block] + [
        swap_within(block, strides, other, batch_size) for other in range(1, factor)
    ]
    return last_kernel(digit, held), done


def body(
    root_state, cond_table, block_gain, w_in, w_out, value_head, reward_head, small_head,
    unroll_len, actions, codes, policy_target, value_bins, reward_bins,
):
    tower_id = lax.axis_index("tower")
    other_id = 1 - tower_id
    tower_ref = tower_id.astype(jnp.int32)[None]
    steps, batch_rows = actions.shape
    blocks, width = block_gain.shape[1:]
    bins = value_head.shape[2]
    table_rows = cond_table.shape[0]
    rows = batch_rows // 2
    half = width // 2
    parts = lax.axis_size("batch")
    s = Sizes(steps, rows, blocks, width, bins, table_rows, parts)
    calls, wide, pair = s.calls, s.wide, s.pair

    root_got = swap(root_state, "tower", 1)
    in_own, out_own, gains_own = w_in[0], w_out[0], block_gain[0]
    value_own = value_head[0].T
    in_got = swap(in_own, "tower", 1)
    out_got = swap(out_own, "tower", 1)
    gains_got = swap(gains_own, "tower", 1)
    value_got = swap(value_own, "tower", 1)
    lengths = unroll_len.reshape(1, batch_rows)

    shape = jax.ShapeDtypeStruct
    per_pair = lambda *tail: pl.BlockSpec(
        (pair,) + tail, lambda turn, tower: (turn,) + (0,) * len(tail)
    )
    forward_params = pltpu.CompilerParams(vmem_limit_bytes=FORWARD_LIMIT)
    backward_params = pltpu.CompilerParams(vmem_limit_bytes=BACKWARD_LIMIT)
    small_params = pltpu.CompilerParams(vmem_limit_bytes=SMALL_LIMIT)
    products = steps * rows * (4 * blocks * width * width + 9 * width * wide)
    cost = pl.CostEstimate(flops=2 * products, bytes_accessed=40 * 2**20, transcendentals=0)
    (
        lat, lat_own, lat_away, entry, after, slope, side, dlat, dlast, loss, head_grads,
        turned, code_rows, gains,
    ) = pl.pallas_call(
        functools.partial(forward_kernel, s),
        grid_spec=pltpu.PrefetchScalarGridSpec(
            num_scalar_prefetch=1,
            grid=(steps // pair,),
            in_specs=[pl.BlockSpec(memory_space=pltpu.HBM)] * 14
            + [pl.BlockSpec(memory_space=pl.ANY)] * 4
            + [whole((blocks, width))],
            out_specs=[
                per_pair(2, rows, width),
                per_pair(rows, width),
                per_pair(rows, width),
                per_pair(calls, rows, width),
                per_pair(calls, rows, width),
                per_pair(calls, rows, width),
                per_pair(calls + 2, rows, LANES),
                pl.BlockSpec(
                    (pair, 2, rows, width), lambda turn, tower: (jnp.maximum(turn - 1, 0), 0, 0, 0)
                ),
                whole((pair, 2, rows, width)),
                whole((8, rows)),
                whole((2, s.head_rows, width)),
                whole((2 * calls, width, width)),
                whole((2, steps, rows)),
                whole((2, 8, width)),
            ],
            scratch_shapes=[
                pltpu.VMEM((rows, half), BF16),
                pltpu.VMEM((rows, half), BF16),
                pltpu.VMEM((1, rows), jnp.int32),
                pltpu.VMEM((steps, rows), jnp.int32),
                pltpu.VMEM((steps, rows), jnp.int32),
                pltpu.VMEM((steps, rows), jnp.int32),
                pltpu.VMEM((steps, 2, rows), jnp.int32),
                pltpu.VMEM((steps, rows), jnp.int32),
                pltpu.VMEM((table_rows, width), BF16),
                pltpu.VMEM((blocks, width), BF16),
                pltpu.VMEM((bins, width), BF16),
                pltpu.VMEM((bins, width), BF16),
                pltpu.VMEM((bins, width), BF16),
                pltpu.VMEM((table_rows, width), BF16),
                pltpu.SemaphoreType.DMA((18,)),
                pltpu.VMEM((rows, width), BF16),
                pltpu.VMEM((pair * rows, width), BF16),
                pltpu.VMEM((pair * rows, width), BF16),
                pltpu.VMEM((LANES, width), BF16),
                pltpu.VMEM((2 * calls, width, width), BF16),
                pltpu.VMEM((s.depth[0], width), BF16),
                pltpu.VMEM((s.depth[1], width), BF16),
                pltpu.VMEM((s.stack[0], width), F32),
                pltpu.VMEM((s.stack[1], width), F32),
                pltpu.VMEM((s.stack[0], pair * rows), F32),
                pltpu.VMEM((s.stack[1], pair * rows), F32),
                pltpu.VMEM((s.depth[0], pair * rows), BF16),
                pltpu.VMEM((s.depth[1], pair * rows), BF16),
                pltpu.VMEM((s.reward_at - s.sums_at, LANES), F32),
                pltpu.VMEM((pair, s.reward_at - s.sums_at, width), F32),
            ],
        ),
        out_shape=[
            shape((steps, 2, rows, width), BF16),
            pltpu.HBM((steps, rows, width), BF16),
            pltpu.HBM((steps, rows, width), BF16),
            shape((steps, calls, rows, width), BF16),
            shape((steps, calls, rows, width), BF16),
            shape((steps, calls, rows, width), F32),
            shape((steps, calls + 2, rows, LANES), F32),
            shape((steps - pair, 2, rows, width), F32),
            shape((pair, 2, rows, width), F32),
            shape((8, rows), F32),
            shape((2, s.head_rows, width), BF16),
            shape((2 * calls, width, width), BF16),
            shape((2, steps, rows), jnp.int32),
            shape((2, 8, width), F32),
        ],
        compiler_params=forward_params,
        cost_estimate=cost,
        name="unroll_forward",
    )(
        tower_ref,
        *[
            pltpu.with_memory_space_constraint(value, pltpu.HBM)
            for value in (
                root_state, lengths, actions, codes, policy_target,
                jnp.swapaxes(value_bins, 0, 1), reward_bins, cond_table, gains_own,
                in_own, out_own, value_own, reward_head.T, small_head.T,
            )
        ],
        root_got, in_got, out_got, value_got, gains_got,
    )

    turns = steps // pair
    descending = lambda *tail: pl.BlockSpec(
        (pair,) + tail, lambda turn, tower: (turns - 1 - turn,) + (0,) * len(tail)
    )
    own, away, root_own, root_away = pl.pallas_call(
        functools.partial(backward_kernel, s),
        grid_spec=pltpu.PrefetchScalarGridSpec(
            num_scalar_prefetch=1,
            grid=(turns,),
            in_specs=[
                descending(2, rows, width),
                descending(calls, rows, width),
                descending(calls, rows, width),
                descending(calls, rows, width),
                descending(calls + 2, rows, LANES),
                pl.BlockSpec(
                    (pair, 2, rows, width),
                    lambda turn, tower: (jnp.minimum(turns - 1 - turn, turns - 2), 0, 0, 0),
                ),
                whole((pair, 2, rows, width)),
                whole((2, steps, rows)),
                whole((2, 8, width)),
                whole((2 * calls, width, width)),
                whole((2, s.head_rows, width)),
            ],
            out_specs=[
                whole((s.total, width)),
                whole((s.total, width)),
                whole((rows, half)),
                whole((rows, half)),
            ],
            scratch_shapes=[
                pltpu.VMEM((rows, width), F32),
                pltpu.VMEM((2, 16, width), F32),
                pltpu.VMEM((s.held, width), F32),
                pltpu.VMEM((2, calls, width, width), F32),
                pltpu.VMEM((2, 16, width), F32),
                pltpu.VMEM((2, 16, width), F32),
                pltpu.VMEM((pair, calls, rows, width), BF16),
                pltpu.VMEM((pair, calls, rows, width), BF16),
                pltpu.VMEM((pair, 2, rows, width), BF16),
            ],
        ),
        out_shape=[
            shape((s.total, width), BF16),
            shape((s.total, width), BF16),
            shape((rows, half), BF16),
            shape((rows, half), BF16),
        ],
        compiler_params=backward_params,
        cost_estimate=cost,
        name="unroll_backward",
    )(
        tower_ref, lat, entry, after, slope, side, dlat, dlast, code_rows, gains,
        turned, head_grads,
    )
    got = swap(away, "tower", 1)

    def beside(given):
        lat_own, lat_away, loss, root_own, root_away = given
        lat_got = swap(lat_away, "tower", 1)
        loss_own = loss[0]
        loss_got = swap(loss_own, "tower", 1)
        root_got = swap(root_away, "tower", 1)

        latents, logits = pl.pallas_call(
            functools.partial(logits_kernel, s),
            grid_spec=pltpu.PrefetchScalarGridSpec(
                num_scalar_prefetch=1,
                grid=(steps // pair,),
                in_specs=[per_pair(rows, width), per_pair(rows, width), whole((bins, width))],
                out_specs=[per_pair(batch_rows, width), per_pair(bins, batch_rows)],
            ),
            out_shape=[
                shape((steps, batch_rows, width), BF16),
                shape((steps, bins, batch_rows), BF16),
            ],
            compiler_params=small_params,
            cost_estimate=pl.CostEstimate(
                flops=2 * steps * batch_rows * width * wide, bytes_accessed=6 * 2**20, transcendentals=0
            ),
            name="latents_and_logits",
        )(
            tower_ref,
            *[
                pltpu.with_memory_space_constraint(part, pltpu.HBM)
                for part in (lat_own, lat_got, value_own)
            ],
        )

        def in_order(mine_value, got_value, axis):
            return jnp.where(
                tower_id == 0,
                jnp.concatenate([mine_value, got_value], axis=axis),
                jnp.concatenate([got_value, mine_value], axis=axis),
            )

        row_loss = in_order(loss_own, loss_got, 0)
        grad_root = in_order(root_own, root_got, 0).astype(F32)
        return latents, logits, row_loss, grad_root

    rounds = exchange_rounds(parts)

    def unpack(digit, held):
        scalars = jnp.stack([digit, tower_id]).astype(jnp.int32)
        length = held[0].shape[0]
        block = s.reward_at // length
        at = s.reward_at - block * length
        parts_of = [part[at : at + s.shared_end - s.reward_at] for part in held]
        shared = parts_of[0]
        for other in range(1, len(held)):
            shared = jnp.where((digit ^ other) == block, parts_of[other], shared)
        shared_got = swap(shared, "tower", 1)
        return (shared, shared_got), pl.pallas_call(
            functools.partial(unpack_own_kernel, s),
            grid_spec=pltpu.PrefetchScalarGridSpec(
                num_scalar_prefetch=1,
                grid=(1,),
                in_specs=[whole(part.shape) for part in held],
                out_specs=[
                    whole((blocks, width, width)),
                    whole((blocks, width, width)),
                    whole((bins, 1, width)),
                    whole((blocks, 1, width)),
                    whole((blocks, 2, steps)),
                ],
                scratch_shapes=[
                    pltpu.VMEM((s.total, width), BF16),
                    pltpu.VMEM((s.reward_at - s.sums_at, LANES), F32),
                ],
            ),
            out_shape=[
                shape((blocks, width, width), F32),
                shape((blocks, width, width), F32),
                shape((bins, 1, width), F32),
                shape((blocks, 1, width), F32),
                shape((blocks, 2, steps), F32),
            ],
            compiler_params=small_params,
            name="unpack_own",
        )(scalars, *held)

    given = (lat_own, lat_away, loss, root_own, root_away)
    unpacked, done = exchange([own, got], rounds, parts, beside, given, unpack)
    (shared, shared_got), (grad_in, grad_out, value_t, gain_t, rms_t) = unpacked
    latents, logits, row_loss, grad_root = done
    reward_t, small_t, grad_cond = pl.pallas_call(
        functools.partial(unpack_shared_kernel, s),
        grid_spec=pltpu.PrefetchScalarGridSpec(
            num_scalar_prefetch=1,
            grid=(1,),
            in_specs=[whole(shared.shape), whole(shared.shape)],
            out_specs=[
                whole((bins, width)),
                whole((table_rows, width)),
                whole((table_rows, width)),
            ],
            scratch_shapes=[pltpu.VMEM((s.wide, width), F32)],
        ),
        out_shape=[
            shape((bins, width), F32),
            shape((table_rows, width), F32),
            shape((table_rows, width), F32),
        ],
        compiler_params=small_params,
        name="unpack_shared",
    )(tower_ref, shared, shared_got)
    layer_rms = jnp.transpose(rms_t, (2, 0, 1))[None]
    return (
        latents[None],
        jnp.swapaxes(logits, 1, 2)[None],
        row_loss,
        layer_rms,
        grad_root,
        grad_cond,
        jnp.swapaxes(gain_t, 0, 1),
        grad_in[None],
        grad_out[None],
        jnp.transpose(value_t, (1, 2, 0)),
        reward_t.T,
        small_t.T,
    )


def solution(mesh):
    placed = (
        P("batch", "tower"),
        P(),
        P("tower", None, None),
        P("tower", None, None, None),
        P("tower", None, None, None),
        P("tower", None, None),
        P(),
        P(),
        P("batch"),
        P(None, "batch"),
        P(None, "batch"),
        P(None, "batch"),
        P(None, None, "batch"),
        P(None, "batch"),
    )
    return jax.shard_map(
        body,
        mesh=mesh,
        in_specs=placed,
        out_specs=(
            P("tower", None, "batch", None),
            P("tower", None, "batch", None),
            P("batch"),
            P("tower", None, None, None),
            P("batch", "tower"),
            P(),
            P("tower", None, None),
            P("tower", None, None, None),
            P("tower", None, None, None),
            P("tower", None, None),
            P(),
            P(),
        ),
        check_vma=False,
    )
```

profile of v0, /device:TPU:9, one launch (start us, length us, event | category | flops | bytes accessed | tf_op | source)
XLA Modules:
  0.0 110.5 jit_solution(5326805046744316114)
XLA Ops:
  0.6 0.7 collective-permute-start.1
  1.4 0.1 collective-permute-start.2
  1.5 0.4 collective-permute-start.3
  1.9 0.1 collective-permute-start
  2.0 0.4 collective-permute-start.4
  2.4 1.6 %collective-permute-done.4.gains_got = bf16[3,256]{1,0:T(4,128)(2,1)S(1)} collective-permute-done((bf16[3,256]{1,0:T(4,128)(2,1)}, bf16[3,256]{1,0:T(4,128)(2,1)S(1)}, u32[]{:S(2)}, u32[]{:S(2)}) %collective-permute-start.4) | collective-permute-done | bytes 1568 | tf_op jit(solution)/shard_map/ppermute | solution.py:610
  4.1 0.0 collective-permute-done.root_any
  4.1 0.0 collective-permute-done.3.value_any
  4.1 0.0 collective-permute-done.1.in_got
  4.1 0.0 collective-permute-done.2.out_got
  4.1 29.9 %unroll_forward.1 = (bf16[10,2,128,256]{3,2,1,0:T(8,128)(2,1)S(1)}, bf16[10,128,256]{2,1,0:T(8,128)(2,1)}, bf16[10,128,256]{2,1,0:T(8,128)(2,1)}, bf16[10,6,128,...) custom-call(s32[1]{0:T(128)} %bitcast.1.tower_ref, ...), custom_call_target="tpu_custom_call" | custom-call | flops 5599395840 | bytes 41943040 | tf_op jit(solution)/shard_map/unroll_forward/pallas_call | solution.py:733
  33.9 20.3 %unroll_backward.1 = (bf16[2560,256]{1,0:T(8,128)(2,1)S(1)}, bf16[2560,256]{1,0:T(8,128)(2,1)}, bf16[128,128]{1,0:T(8,128)(2,1)S(1)}, bf16[128,128]{1,0:T(8,128)(2,1)S(1)}) custom-call(s32[1]{0:T(128)} %bitcast.1.tower_ref, bf16[10,2,128,256]{3,2,1,0:T(8,128)(2,1)S(1)} %get-tuple-element.61.lat, bf16[10,6,128,256]{3,2,1,0:T(8,128)(2,1)S(1)} %get-tuple-element.62.entry, ...), custom_call_target="tpu_custom_call" | custom-call | flops 5599395840 | bytes 41943040 | tf_op jit(solution)/shard_map/unroll_backward/pallas_call | solution.py:828
  54.2 0.4 collective-permute-start.5
  54.6 2.9 %collective-permute-done.5 = bf16[2560,256]{1,0:T(8,128)(2,1)S(1)} collective-permute-done((bf16[2560,256]{1,0:T(8,128)(2,1)}, bf16[2560,256]{1,0:T(8,128)(2,1)S(1)}, u32[]{:S(2)}, u32[]{:S(2)}) %collective-permute-start.5) | collective-permute-done | bytes 1310752 | tf_op jit(solution)/shard_map/ppermute | solution.py:610
  57.5 1.3 %add_and_split.1 = (bf16[640,256]{1,0:T(8,128)(2,1)}, bf16[640,256]{1,0:T(8,128)(2,1)}, bf16[640,256]{1,0:T(8,128)(2,1)}, bf16[640,256]{1,0:T(8,128)(2,1)}) custom-call(s32[1]{0:T(128)} %bitcast.digit_ref, bf16[4,640,256]{2,1,0:T(8,128)(2,1)S(1)} %bitcast.29, bf16[4,640,256]{2,1,0:T(8,128)(2,1)S(1)} %bitcast.30), custom_call_target="tpu_custom_call" | custom-call | tf_op jit(solution)/shard_map/add_and_split/pallas_call | solution.py:664
  58.7 0.4 collective-permute-start.9
  59.1 0.0 collective-permute-start.6
  59.1 2.5 %collective-permute-start.7 = (bf16[640,256]{1,0:T(8,128)(2,1)}, bf16[640,256]{1,0:T(8,128)(2,1)S(1)}, u32[]{:S(2)}, u32[]{:S(2)}) collective-permute-start(bf16[640,256]{1,0:T(8,128)(2,1)} %get-tuple-element.85), channel_id=1, source_target_pairs={{0,2},{1,3},{2,0},{3,1},{4,6},{5,7},{6,4},{7,5},{8,10},{9,11},{10,... | collective-permute-start | bytes 983048 | tf_op jit(solution)/shard_map/ppermute | solution.py:635
  61.6 0.2 collective-permute-start.8
  61.8 1.0 collective-permute-start.10
  62.7 0.8 collective-permute-done.10
  63.6 0.3 collective-permute-start.11
  63.9 0.6 maximum_select_fusion.1
  64.4 0.3 collective-permute-done.11
  64.8 0.7 fusion.2
  65.4 0.0 collective-permute-done.9.lat_got
  65.4 0.8 copy-done.2
  66.3 5.7 %latents_and_logits.1 = (bf16[10,256,256]{2,1,0:T(8,128)(2,1)}, bf16[10,601,256]{2,1,0:T(8,128)(2,1)}) custom-call(s32[1]{0:T(128)} %bitcast.1.tower_ref, bf16[10,128,256]{2,1,0:T(8,128)(2,1)} %get-tuple-element.87.lat_own, bf16[10,128,256]{2,1,0:T(8,128)(2,1)} %copy-done.2, bf16[601,256]{1,0:T(8,128)(2,1)} %bitcast.42), custom_call_target="tpu_custom_call" | custom-call | flops 796917760 | bytes 6291456 | tf_op jit(solution)/shard_map/latents_and_logits/pallas_call | solution.py:889
  72.0 0.0 collective-permute-done.6.refs_1_
  72.0 1.0 collective-permute-done.7.refs_2_
  73.0 4.3 %collective-permute-done.8.refs_3_ = bf16[640,256]{1,0:T(8,128)(2,1)S(1)} collective-permute-done((bf16[640,256]{1,0:T(8,128)(2,1)}, bf16[640,256]{1,0:T(8,128)(2,1)S(1)}, u32[]{:S(2)}, u32[]{:S(2)}) %collective-permute-start.8) | collective-permute-done | bytes 327712 | tf_op jit(solution)/shard_map/ppermute | solution.py:635
  77.3 0.2 add_up.3.refs_0_
  77.5 1.3 %collective-permute-start.12 = (bf16[640,256]{1,0:T(8,128)(2,1)S(1)}, bf16[640,256]{1,0:T(8,128)(2,1)S(1)}, u32[]{:S(2)}, u32[]{:S(2)}) collective-permute-start(bf16[640,256]{1,0:T(8,128)(2,1)S(1)} %add_up.3.refs_0_), channel_id=1, source_target_pairs={{0,4},{1,5},{2,6},{3,7},{4,0},{5,1},{6,2},{7,3},{8,12},{9,13},{10,... | collective-permute-start | bytes 983048 | tf_op jit(solution)/shard_map/ppermute | solution.py:635
  78.8 4.7 %collective-permute-done.12.refs_1_ = bf16[640,256]{1,0:T(8,128)(2,1)S(1)} collective-permute-done((bf16[640,256]{1,0:T(8,128)(2,1)S(1)}, bf16[640,256]{1,0:T(8,128)(2,1)S(1)}, u32[]{:S(2)}, u32[]{:S(2)}) %collective-permute-start.12) | collective-permute-done | bytes 327712 | tf_op jit(solution)/shard_map/ppermute | solution.py:635
  83.5 0.1 add_up.4.refs_0_
  83.6 1.3 %collective-permute-start.13 = (bf16[640,256]{1,0:T(8,128)(2,1)S(1)}, bf16[640,256]{1,0:T(8,128)(2,1)S(1)}, u32[]{:S(2)}, u32[]{:S(2)}) collective-permute-start(bf16[640,256]{1,0:T(8,128)(2,1)S(1)} %add_up.4.refs_0_), channel_id=1, source_target_pairs={{0,8},{1,9},{2,10},{3,11},{4,12},{5,13},{6,14},{7,15},{8,0},{9,1},... | collective-permute-start | bytes 983048 | tf_op jit(solution)/shard_map/ppermute | solution.py:635
  84.9 4.7 %collective-permute-done.13.refs_1_ = bf16[640,256]{1,0:T(8,128)(2,1)S(1)} collective-permute-done((bf16[640,256]{1,0:T(8,128)(2,1)S(1)}, bf16[640,256]{1,0:T(8,128)(2,1)S(1)}, u32[]{:S(2)}, u32[]{:S(2)}) %collective-permute-start.13) | collective-permute-done | bytes 327712 | tf_op jit(solution)/shard_map/ppermute | solution.py:635
  89.5 0.1 add_up.5.refs_0_
  89.6 0.1 collective-permute-start.14
  89.7 2.5 %collective-permute-start.15 = (bf16[640,256]{1,0:T(8,128)(2,1)S(1)}, bf16[640,256]{1,0:T(8,128)(2,1)S(1)}, u32[]{:S(2)}, u32[]{:S(2)}) collective-permute-start(bf16[640,256]{1,0:T(8,128)(2,1)S(1)} %add_up.5.refs_0_), channel_id=1, source_target_pairs={{0,2},{1,3},{2,0},{3,1},{4,6},{5,7},{6,4},{7,5},{8,10},{9,11},{10,... | collective-permute-start | bytes 983048 | tf_op jit(solution)/shard_map/ppermute | solution.py:635
  92.2 0.2 collective-permute-start.16
  92.3 4.8 %collective-permute-done.14.refs_1_ = bf16[640,256]{1,0:T(8,128)(2,1)S(1)} collective-permute-done((bf16[640,256]{1,0:T(8,128)(2,1)S(1)}, bf16[640,256]{1,0:T(8,128)(2,1)S(1)}, u32[]{:S(2)}, u32[]{:S(2)}) %collective-permute-start.14) | collective-permute-done | bytes 327712 | tf_op jit(solution)/shard_map/ppermute | solution.py:635
  97.1 6.1 %collective-permute-done.15.refs_2_ = bf16[640,256]{1,0:T(8,128)(2,1)S(1)} collective-permute-done((bf16[640,256]{1,0:T(8,128)(2,1)S(1)}, bf16[640,256]{1,0:T(8,128)(2,1)S(1)}, u32[]{:S(2)}, u32[]{:S(2)}) %collective-permute-start.15) | collective-permute-done | bytes 327712 | tf_op jit(solution)/shard_map/ppermute | solution.py:635
  103.3 4.1 %collective-permute-done.16.refs_3_ = bf16[640,256]{1,0:T(8,128)(2,1)S(1)} collective-permute-done((bf16[640,256]{1,0:T(8,128)(2,1)S(1)}, bf16[640,256]{1,0:T(8,128)(2,1)S(1)}, u32[]{:S(2)}, u32[]{:S(2)}) %collective-permute-start.16) | collective-permute-done | bytes 327712 | tf_op jit(solution)/shard_map/ppermute | solution.py:635
  107.4 0.1 collective-permute-start.17
  107.5 0.1 pad_add_fusion.scalars
  107.6 2.0 %unpack_own.1 = (f32[3,256,256]{2,1,0:T(8,128)}, f32[3,256,256]{2,1,0:T(8,128)}, f32[601,1,256]{2,1,0:T(1,128)}, f32[3,1,256]{2,1,0:T(1,128)}, f32[3,2,10]{2,1,0:T(2,128)}) custom-call(s32[2]{0:T(128)S(1)} %pad_add_fusion.scalars, bf16[640,256]{1,0:T(8,128)(2,1)S(1)} %add_up.5.refs_0_, bf16[640,256]{1,0:T(8,128)(2,1)S(1)} %collective-permute-done.14.refs_1_, ...), custom_call_target="tpu_custom_call" | custom-call | tf_op jit(solution)/shard_map/unpack_own/pallas_call | solution.py:937
  109.6 0.9 unpack_shared.1
  (8 shorter events, 0.1 us)
Async XLA Ops:
  0.6 3.4 %collective-permute-start.1 = (bf16[3,256,256]{2,1,0:T(8,128)(2,1)}, bf16[3,256,256]{2,1,0:T(8,128)(2,1)S(1)}, u32[]{:S(2)}, u32[]{:S(2)}) collective-permute-start(bf16[3,256,256]{2,1,0:T(8,128)(2,1)} %bitcast.35), channel_id=1, source_target_pairs={{0,16},{16,0},{1,17},{17,1},{2,18},{18,2},{3,19},{19,3},{4,20},{20... | collective-permute-start | bytes 1179656 | tf_op jit(solution)/shard_map/ppermute | solution.py:610
  1.4 2.7 %collective-permute-start.2 = (bf16[3,256,256]{2,1,0:T(8,128)(2,1)}, bf16[3,256,256]{2,1,0:T(8,128)(2,1)S(1)}, u32[]{:S(2)}, u32[]{:S(2)}) collective-permute-start(bf16[3,256,256]{2,1,0:T(8,128)(2,1)} %bitcast.37), channel_id=1, source_target_pairs={{0,16},{16,0},{1,17},{17,1},{2,18},{18,2},{3,19},{19,3},{4,20},{20... | collective-permute-start | bytes 1179656 | tf_op jit(solution)/shard_map/ppermute | solution.py:610
  1.5 2.6 %collective-permute-start.3 = (bf16[601,256]{1,0:T(8,128)(2,1)}, bf16[601,256]{1,0:T(8,128)(2,1)S(1)}, u32[]{:S(2)}, u32[]{:S(2)}) collective-permute-start(bf16[601,256]{1,0:T(8,128)(2,1)} %bitcast.40), channel_id=1, source_target_pairs={{0,16},{16,0},{1,17},{17,1},{2,18},{18,2},{3,19},{19,3},{4,20},{20... | collective-permute-start | bytes 923144 | tf_op jit(solution)/shard_map/ppermute | solution.py:610
  1.9 2.2 %collective-permute-start = (bf16[256,128]{1,0:T(8,128)(2,1)}, bf16[256,128]{1,0:T(8,128)(2,1)S(1)}, u32[]{:S(2)}, u32[]{:S(2)}) collective-permute-start(bf16[256,128]{1,0:T(8,128)(2,1)} %root_hbm.1), channel_id=1, source_target_pairs={{0,16},{16,0},{1,17},{17,1},{2,18},{18,2},{3,19},{19,3},{4,20},{20... | collective-permute-start | bytes 196616 | tf_op jit(solution)/shard_map/ppermute | solution.py:610
  2.0 2.1 %collective-permute-start.4 = (bf16[3,256]{1,0:T(4,128)(2,1)}, bf16[3,256]{1,0:T(4,128)(2,1)S(1)}, u32[]{:S(2)}, u32[]{:S(2)}) collective-permute-start(bf16[3,256]{1,0:T(4,128)(2,1)} %bitcast.48), channel_id=1, source_target_pairs={{0,16},{16,0},{1,17},{17,1},{2,18},{18,2},{3,19},{19,3},{4,20},{20... | collective-permute-start | bytes 4616 | tf_op jit(solution)/shard_map/ppermute | solution.py:610
  54.2 4.5 %copy-start.1 = (bf16[10,128,256]{2,1,0:T(8,128)(2,1)S(1)}, bf16[10,128,256]{2,1,0:T(8,128)(2,1)}, u32[]{:S(2)}) copy-start(bf16[10,128,256]{2,1,0:T(8,128)(2,1)} %get-tuple-element.88) | copy-start | bytes 1966084
  54.2 3.2 %collective-permute-start.5 = (bf16[2560,256]{1,0:T(8,128)(2,1)}, bf16[2560,256]{1,0:T(8,128)(2,1)S(1)}, u32[]{:S(2)}, u32[]{:S(2)}) collective-permute-start(bf16[2560,256]{1,0:T(8,128)(2,1)} %get-tuple-element.73), channel_id=1, source_target_pairs={{0,16},{16,0},{1,17},{17,1},{2,18},{18,2},{3,19},{19,3},{4,20},{20... | collective-permute-start | bytes 3932168 | tf_op jit(solution)/shard_map/ppermute | solution.py:610
  58.7 18.6 %copy-start = (bf16[640,256]{1,0:T(8,128)(2,1)S(1)}, bf16[640,256]{1,0:T(8,128)(2,1)}, u32[]{:S(2)}) copy-start(bf16[640,256]{1,0:T(8,128)(2,1)} %get-tuple-element.97.refs_0_) | copy-start | bytes 983044
  58.7 6.7 %collective-permute-start.9 = (bf16[10,128,256]{2,1,0:T(8,128)(2,1)S(1)}, bf16[10,128,256]{2,1,0:T(8,128)(2,1)S(1)}, u32[]{:S(2)}, u32[]{:S(2)}) collective-permute-start(bf16[10,128,256]{2,1,0:T(8,128)(2,1)S(1)} %copy-done.1), channel_id=1, source_target_pairs={{0,16},{16,0},{1,17},{17,1},{2,18},{18,2},{3,19},{19,3},{4,20},{20... | collective-permute-start | bytes 1966088 | tf_op jit(solution)/shard_map/ppermute | solution.py:610
  59.1 12.9 %collective-permute-start.6 = (bf16[640,256]{1,0:T(8,128)(2,1)}, bf16[640,256]{1,0:T(8,128)(2,1)S(1)}, u32[]{:S(2)}, u32[]{:S(2)}) collective-permute-start(bf16[640,256]{1,0:T(8,128)(2,1)} %get-tuple-element.84), channel_id=1, source_target_pairs={{0,1},{1,0},{2,3},{3,2},{4,5},{5,4},{6,7},{7,6},{8,9},{9,8},{10,11... | collective-permute-start | bytes 983048 | tf_op jit(solution)/shard_map/ppermute | solution.py:635
  59.1 13.9 %collective-permute-start.7 = (bf16[640,256]{1,0:T(8,128)(2,1)}, bf16[640,256]{1,0:T(8,128)(2,1)S(1)}, u32[]{:S(2)}, u32[]{:S(2)}) collective-permute-start(bf16[640,256]{1,0:T(8,128)(2,1)} %get-tuple-element.85), channel_id=1, source_target_pairs={{0,2},{1,3},{2,0},{3,1},{4,6},{5,7},{6,4},{7,5},{8,10},{9,11},{10,... | collective-permute-start | bytes 983048 | tf_op jit(solution)/shard_map/ppermute | solution.py:635
  61.6 15.7 %collective-permute-start.8 = (bf16[640,256]{1,0:T(8,128)(2,1)}, bf16[640,256]{1,0:T(8,128)(2,1)S(1)}, u32[]{:S(2)}, u32[]{:S(2)}) collective-permute-start(bf16[640,256]{1,0:T(8,128)(2,1)} %get-tuple-element.86), channel_id=1, source_target_pairs={{0,3},{1,2},{2,1},{3,0},{4,7},{5,6},{6,5},{7,4},{8,11},{9,10},{10,... | collective-permute-start | bytes 983048 | tf_op jit(solution)/shard_map/ppermute | solution.py:635
  61.8 1.8 %collective-permute-start.10 = (f32[128]{0:T(128)S(1)}, f32[128]{0:T(128)S(1)}, u32[]{:S(2)}, u32[]{:S(2)}) collective-permute-start(f32[128]{0:T(128)S(1)} %slice_bitcast_fusion), channel_id=1, source_target_pairs={{0,16},{16,0},{1,17},{17,1},{2,18},{18,2},{3,19},{19,3},{4,20},{20... | collective-permute-start | bytes 1544 | tf_op jit(solution)/shard_map/ppermute | solution.py:610
  63.6 1.2 %collective-permute-start.11 = (bf16[128,128]{1,0:T(8,128)(2,1)S(1)}, bf16[128,128]{1,0:T(8,128)(2,1)S(1)}, u32[]{:S(2)}, u32[]{:S(2)}) collective-permute-start(bf16[128,128]{1,0:T(8,128)(2,1)S(1)} %get-tuple-element.93), channel_id=1, source_target_pairs={{0,16},{16,0},{1,17},{17,1},{2,18},{18,2},{3,19},{19,3},{4,20},{20... | collective-permute-start | bytes 98312 | tf_op jit(solution)/shard_map/ppermute | solution.py:610
  65.4 0.8 copy-start.2
  77.5 6.0 %collective-permute-start.12 = (bf16[640,256]{1,0:T(8,128)(2,1)S(1)}, bf16[640,256]{1,0:T(8,128)(2,1)S(1)}, u32[]{:S(2)}, u32[]{:S(2)}) collective-permute-start(bf16[640,256]{1,0:T(8,128)(2,1)S(1)} %add_up.3.refs_0_), channel_id=1, source_target_pairs={{0,4},{1,5},{2,6},{3,7},{4,0},{5,1},{6,2},{7,3},{8,12},{9,13},{10,... | collective-permute-start | bytes 983048 | tf_op jit(solution)/shard_map/ppermute | solution.py:635
  83.6 6.0 %collective-permute-start.13 = (bf16[640,256]{1,0:T(8,128)(2,1)S(1)}, bf16[640,256]{1,0:T(8,128)(2,1)S(1)}, u32[]{:S(2)}, u32[]{:S(2)}) collective-permute-start(bf16[640,256]{1,0:T(8,128)(2,1)S(1)} %add_up.4.refs_0_), channel_id=1, source_target_pairs={{0,8},{1,9},{2,10},{3,11},{4,12},{5,13},{6,14},{7,15},{8,0},{9,1},... | collective-permute-start | bytes 983048 | tf_op jit(solution)/shard_map/ppermute | solution.py:635
  89.6 7.5 %collective-permute-start.14 = (bf16[640,256]{1,0:T(8,128)(2,1)S(1)}, bf16[640,256]{1,0:T(8,128)(2,1)S(1)}, u32[]{:S(2)}, u32[]{:S(2)}) collective-permute-start(bf16[640,256]{1,0:T(8,128)(2,1)S(1)} %add_up.5.refs_0_), channel_id=1, source_target_pairs={{0,1},{1,0},{2,3},{3,2},{4,5},{5,4},{6,7},{7,6},{8,9},{9,8},{10,11... | collective-permute-start | bytes 983048 | tf_op jit(solution)/shard_map/ppermute | solution.py:635
  89.7 13.6 %collective-permute-start.15 = (bf16[640,256]{1,0:T(8,128)(2,1)S(1)}, bf16[640,256]{1,0:T(8,128)(2,1)S(1)}, u32[]{:S(2)}, u32[]{:S(2)}) collective-permute-start(bf16[640,256]{1,0:T(8,128)(2,1)S(1)} %add_up.5.refs_0_), channel_id=1, source_target_pairs={{0,2},{1,3},{2,0},{3,1},{4,6},{5,7},{6,4},{7,5},{8,10},{9,11},{10,... | collective-permute-start | bytes 983048 | tf_op jit(solution)/shard_map/ppermute | solution.py:635
  92.2 15.2 %collective-permute-start.16 = (bf16[640,256]{1,0:T(8,128)(2,1)S(1)}, bf16[640,256]{1,0:T(8,128)(2,1)S(1)}, u32[]{:S(2)}, u32[]{:S(2)}) collective-permute-start(bf16[640,256]{1,0:T(8,128)(2,1)S(1)} %add_up.5.refs_0_), channel_id=1, source_target_pairs={{0,3},{1,2},{2,1},{3,0},{4,7},{5,6},{6,5},{7,4},{8,11},{9,10},{10,... | collective-permute-start | bytes 983048 | tf_op jit(solution)/shard_map/ppermute | solution.py:635
  107.4 2.2 %collective-permute-start.17 = (bf16[400,256]{1,0:T(8,128)(2,1)S(1)}, bf16[400,256]{1,0:T(8,128)(2,1)S(1)}, u32[]{:S(2)}, u32[]{:S(2)}) collective-permute-start(bf16[400,256]{1,0:T(8,128)(2,1)S(1)} %fusion.1.mine), channel_id=1, source_target_pairs={{0,16},{16,0},{1,17},{17,1},{2,18},{18,2},{3,19},{19,3},{4,20},{20... | collective-permute-start | bytes 614408 | tf_op jit(solution)/shard_map/ppermute | solution.py:610
where the time goes:
time: 111 us
  Pallas kernels  60.4 us (54%)
  waiting for transfers between devices  35.4 us (32%)
  starting transfers between devices  11.8 us (11%)
  other arithmetic  1.36 us (1%)
    pallas_call x1, Pallas kernels, body(): pl.pallas_call(functools.partial(forward_kernel, s), grid_spec=pltpu.Pref...  29.9 us
    ppermute x8, waiting for transfers between devices, swap_within(): return lax.ppermute(value, AXES, pairs)  29.8 us
    pallas_call x1, Pallas kernels, body(): pl.pallas_call(functools.partial(backward_kernel, s), grid_spec=pltpu.Pre...  20.3 us
    ppermute x8, starting transfers between devices, swap_within(): return lax.ppermute(value, AXES, pairs)  7.93 us
    pallas_call x1, Pallas kernels, beside(): pl.pallas_call(functools.partial(logits_kernel, s), grid_spec=pltpu.Prefe...  5.7 us
    ppermute x10, waiting for transfers between devices, swap(): return lax.ppermute(value, axis, pairs)  5.69 us
    ppermute x10, starting transfers between devices, swap(): return lax.ppermute(value, axis, pairs)  3.85 us
  transfers between devices with their start and end apart: 18, of which 11 were waited for; matrix products, arithmetic and copies ran while one was open for 1% of the time, Pallas kernels for 7%

commit v1 on v0

--- a/solution.py
+++ b/solution.py
@@ -10,8 +10,7 @@
 ACTIONS = 4
 LANES = 128
 MIB = 1024 * 1024
-FORWARD_LIMIT = 20 * MIB
-BACKWARD_LIMIT = 20 * MIB
+UNROLL_LIMIT = 46 * MIB
 SMALL_LIMIT = 12 * MIB
 epsilon = 1e-06
 very_negative = -1e30
@@ -82,12 +81,53 @@
         self.head_rows = self.cond_at - self.value_at
 
 
-def forward_kernel(
+def unroll_kernel(
     sizes, tower_ref,
     root_hbm, lengths_hbm, actions_hbm, codes_hbm, policy_hbm, value_bins_hbm, reward_bins_hbm,
     table_hbm, gains_hbm, in_hbm, out_hbm, value_hbm, reward_hbm, small_hbm,
     root_any, in_got, out_got, value_any, gains_got,
-    lat, lat_own, lat_away, entry, after, slope, side, dlat, dlast, loss, head_grads, turned, code_rows, gains,
+    lat_own, lat_away, loss, own, away, root_own_grad, root_away_grad,
+    lat, entry, after, slope, side, dlat, turned, gains,
+    root_own, root_got, lengths, actions, codes, policy, value_bins, reward_bins,
+    table_in, gains_own, value_own, value_got, reward_in, small_in, sems,
+    state, past0, past1, table, weights, heads0, heads1, acc0, acc1,
+    logits0, logits1, cot0, cot1, sums, squares,
+    carry, gain_sum, cond_sum, grads, inverse_gains, d_after_kept, d_before_kept, d_hidden_kept,
+):
+    turn = pl.program_id(0)
+    turns = sizes.steps // sizes.pair
+
+    @pl.when(turn < turns)
+    def _():
+        forward_turn(
+            sizes, turn, tower_ref,
+            root_hbm, lengths_hbm, actions_hbm, codes_hbm, policy_hbm, value_bins_hbm,
+            reward_bins_hbm, table_hbm, gains_hbm, in_hbm, out_hbm, value_hbm, reward_hbm,
+            small_hbm, root_any, in_got, out_got, value_any, gains_got,
+            lat, lat_own, lat_away, entry, after, slope, side, dlat, loss, turned, gains,
+            root_own, root_got, lengths, actions, codes, policy, value_bins, reward_bins,
+            table_in, gains_own, value_own, value_got, reward_in, small_in, sems,
+            state, past0, past1, table, weights, heads0, heads1, acc0, acc1,
+            logits0, logits1, cot0, cot1, sums, squares,
+        )
+
+    @pl.when(turn >= turns)
+    def _():
+        backward_turn(
+            sizes, turn - turns, tower_ref,
+            lat, entry, after, slope, side, dlat, actions, codes, turned, acc0, acc1, sums,
+            own, away, root_own_grad, root_away_grad,
+            carry, gain_sum, cond_sum, grads, gains, inverse_gains, d_after_kept, d_before_kept,
+            d_hidden_kept,
+        )
+
+
+def forward_turn(
+    sizes, turn, tower_ref,
+    root_hbm, lengths_hbm, actions_hbm, codes_hbm, policy_hbm, value_bins_hbm, reward_bins_hbm,
+    table_hbm, gains_hbm, in_hbm, out_hbm, value_hbm, reward_hbm, small_hbm,
+    root_any, in_got, out_got, value_any, gains_got,
+    lat, lat_own, lat_away, entry, after, slope, side, dlat, loss, turned, gains,
     root_own, root_got, lengths, actions, codes, policy, value_bins, reward_bins,
     table_in, gains_own, value_own, value_got, reward_in, small_in, sems,
     state, past0, past1, table, weights, heads0, heads1, acc0, acc1,
@@ -95,7 +135,6 @@
 ):
     s = sizes
     pair = s.pair
-    turn = pl.program_id(0)
     first_step = turn * pair
     tower_id = tower_ref[0]
     rows, width, wide = s.rows, s.width, s.wide
@@ -133,15 +172,14 @@
         ]
         for move in moves:
             move.start()
+        gains[...] = jnp.ones_like(gains)
         for target in (
-            gains, table, heads0, heads1, past0, past1, cot0, cot1, acc0, acc1, sums, squares, loss
+            table, heads0, heads1, past0, past1, cot0, cot1, acc0, acc1, sums, squares, loss
         ):
             target[...] = jnp.zeros_like(target)
         for move in moves:
             move.wait()
         first = tower_id == 0
-        code_rows[0] = actions[...]
-        code_rows[1] = codes[...] + ACTIONS
         state[:, 0 : width // 2] = jnp.where(first, root_own[...], root_got[...])
         state[:, width // 2 : width] = jnp.where(first, root_got[...], root_own[...])
         gains[tower_id, 0 : s.blocks, :] = gains_own[...].astype(F32)
@@ -242,7 +280,7 @@
         def make_latent():
             d_latent = by_rows(cot[...], stack[...])
             for offset in range(pair):
-                put[offset, tower] = d_latent[offset * rows : (offset + 1) * rows]
+                put[at_step + offset, tower] = d_latent[offset * rows : (offset + 1) * rows]
 
         large = cuts(acc.shape[0], 320)
         pieces = [functools.partial(make_logits, *cut) for cut in large]
@@ -298,8 +336,8 @@
             chain["product"] = natural(gained.astype(BF16), weights[place])
             row_squares, inv_scale = scale_rows()
             chain["scale"] = inv_scale
-            entry[offset, place] = (gained * inv_scale).astype(BF16)
-            side[offset, place] = jnp.broadcast_to(inv_scale, (rows, LANES))
+            entry[first_step + offset, place] = (gained * inv_scale).astype(BF16)
+            side[first_step + offset, place] = jnp.broadcast_to(inv_scale, (rows, LANES))
             if block > 0:
                 keep_squares(block - 1, row_squares)
                 keep_branch(block - 1, branch)
@@ -310,8 +348,8 @@
             gate = 0.5 * jnp.tanh(0.5 * u) + 0.5
             after_rows = (u * gate).astype(BF16)
             chain["product"] = natural(after_rows, weights[s.calls + place])
-            after[offset, place] = after_rows
-            slope[offset, place] = gate * (1.0 + u * (1.0 - gate))
+            after[first_step + offset, place] = after_rows
+            slope[first_step + offset, place] = gate * (1.0 + u * (1.0 - gate))
 
         def finish():
             branch = end_block(s.blocks - 1)
@@ -323,8 +361,8 @@
                 chain["hidden"] = latent.astype(F32) + chain[following]
 
             def keep():
-                side[offset, s.calls + tower] = jnp.broadcast_to(inv_scale, (rows, LANES))
-                lat[offset, tower] = latent
+                side[first_step + offset, s.calls + tower] = jnp.broadcast_to(inv_scale, (rows, LANES))
+                lat[first_step + offset, tower] = latent
                 keep_squares(s.blocks - 1, row_squares)
                 keep_branch(s.blocks - 1, branch)
                 if tower == 0:
@@ -389,42 +427,27 @@
         total = lane_sum(squares[offset])
         sums[...] = jnp.where(at_lane == first_step + offset, total, sums[...])
 
-    @pl.when(turn == pl.num_programs(0) - 1)
+    @pl.when(turn == s.steps // pair - 1)
     def _():
         live_now = live_rows(first_step)
-        weave(heads(1, live_now, first_step, dlast), heads(0, live_now, first_step, dlast))
-        half = wide // 2
-        head_grads[...] = jnp.zeros_like(head_grads)
-        head_grads[0, 0:wide, :] = acc0[0:wide, :].astype(BF16)
-        head_grads[1, 0:wide, :] = acc1[0:wide, :].astype(BF16)
-        small = acc0[wide : wide + s.held, :] + acc1[2 * wide : 2 * wide + s.held, :]
-        at = s.small_at - s.value_at
-        head_grads[0, at : at + s.held, :] = small.astype(BF16)
-        for tower in range(2):
-            put = s.reward_at - s.value_at
-            at = wide + tower * half
-            head_grads[tower, put : put + half, :] = acc1[at : at + half, :].astype(BF16)
-            head_grads[tower, wide : wide + sums.shape[0], 0:LANES] = sums[...].astype(BF16)
-
-
-def backward_kernel(
-    sizes, tower_ref,
-    lat, entry, after, slope, side, dlat, dlast, code_rows, gains_in, turned, head_grads,
+        weave(heads(1, live_now, first_step, dlat), heads(0, live_now, first_step, dlat))
+
+
+def backward_turn(
+    sizes, turn, tower_ref,
+    lat, entry, after, slope, side, dlat, actions, codes, turned, acc0, acc1, sums,
     own, away, root_own, root_away,
     carry, gain_sum, cond_sum, grads, gains, inverse_gains, d_after_kept, d_before_kept,
     d_hidden_kept,
 ):
     s = sizes
     pair = s.pair
-    turn = pl.program_id(0)
     first_step = s.steps - pair * (turn + 1)
     tower_id = tower_ref[0]
     blocks, width = s.blocks, s.width
 
     @pl.when(turn == 0)
     def _():
-        gains[...] = jnp.ones_like(gains)
-        gains[:, 0:blocks, :] = gains_in[:, 0:blocks, :]
         inverse_gains[...] = 1.0 / gains[...]
         carry[...] = jnp.zeros_like(carry)
         grads[...] = jnp.zeros_like(grads)
@@ -440,15 +463,16 @@
     def add_grads(matrix, rows_of, place, kept, now):
         later = [kept[offset, place] for offset in range(1, pair)]
         grads[matrix // s.calls, matrix % s.calls] += by_rows(
-            stacked([rows_of[offset, place] for offset in range(pair)]), stacked([now] + later)
+            stacked([rows_of[first_step + offset, place] for offset in range(pair)]), stacked([now] + later)
         )
 
     def add_cond(offset, tower, d_hidden):
         if offset > 0:
             d_hidden_kept[offset, tower] = d_hidden.astype(BF16)
             return
+        codes_of, shift = (actions, 0) if tower == 0 else (codes, ACTIONS)
         code = jnp.concatenate(
-            [code_rows[tower, pl.ds(first_step + step, 1), :] for step in range(pair)], axis=1
+            [codes_of[pl.ds(first_step + step, 1), :] + shift for step in range(pair)], axis=1
         )
         spots = lax.broadcasted_iota(jnp.int32, (cond_sum.shape[0], pair * s.rows), 0)
         onehot = jnp.where(spots == code, 1.0, 0.0).astype(BF16)
@@ -463,9 +487,9 @@
             behind.pop(0)()
 
     def tower_back(offset, tower, d_latent):
-        normed = lat[offset, tower]
+        normed = lat[first_step + offset, tower]
         normed_wide = normed.astype(F32)
-        inv_scale = over_lanes(side[offset, s.calls + tower])
+        inv_scale = over_lanes(side[first_step + offset, s.calls + tower])
         base = inv_scale * d_latent
         slant = inv_scale * (lane_sum(d_latent * normed_wide) * (1.0 / width))
         for block in reversed(range(blocks)):
@@ -476,11 +500,11 @@
             )
             d_hidden = base - slant * normed_wide
             d_branch = d_hidden.astype(BF16)
-            entry_wide = entry[offset, place].astype(F32)
-            inv_scale = over_lanes(side[offset, place])
+            entry_wide = entry[first_step + offset, place].astype(F32)
+            inv_scale = over_lanes(side[first_step + offset, place])
             catch_up()
             d_after = both[s.rows :] - slant * both[: s.rows]
-            d_before = (d_after * slope[offset, place]).astype(BF16)
+            d_before = (d_after * slope[first_step + offset, place]).astype(BF16)
             d_entry = natural(d_before, turned[place])
             if offset > 0:
                 d_after_kept[offset, place] = d_branch
@@ -506,35 +530,54 @@
         return d_hidden
 
     def from_heads(offset, tower):
-        return jnp.where(turn == 0, dlast[offset, tower], dlat[offset, tower])
+        return jnp.where(turn == 0, dlast[offset, tower], dlat[first_step + offset, tower])
 
     d_state = carry[...]
     for offset in reversed(range(pair)):
         for tower in (1, 0):
-            d_state = tower_back(offset, tower, d_state + from_heads(offset, tower))
+            d_state = tower_back(offset, tower, d_state + dlat[first_step + offset, tower])
     catch_up()
     carry[...] = d_state
 
-    @pl.when(turn == pl.num_programs(0) - 1)
+    @pl.when(turn == s.steps // pair - 1)
     def _():
         left = d_state[:, 0 : width // 2].astype(BF16)
         right = d_state[:, width // 2 : width].astype(BF16)
         root_own[...] = jnp.where(tower_id == 0, left, right)
         root_away[...] = jnp.where(tower_id == 0, right, left)
         gain_sum[...] = gain_sum[...] * inverse_gains[...]
-        lines = lax.broadcasted_iota(jnp.int32, (s.reward_at - s.sums_at, width), 0)
+        wide, half = s.wide, s.wide // 2
+        lines = lax.broadcasted_iota(jnp.int32, sums.shape, 0)
+        small = acc0[wide : wide + s.held, :] + acc1[2 * wide : 2 * wide + s.held, :]
         for target, which in ((own, tower_id), (away, 1 - tower_id)):
+            first = which == 0
             for matrix in range(s.calls):
                 at = matrix * width
                 target[at : at + width, :] = grads[which, matrix].astype(BF16)
-            target[s.value_at : s.cond_at, :] = head_grads[which]
-            sums = head_grads[which, s.wide : s.wide + lines.shape[0], :].astype(F32)
+            for start, stop in cuts(wide):
+                value = jnp.where(first, acc0[start:stop, :], acc1[start:stop, :])
+                target[s.value_at + start : s.value_at + stop, :] = value.astype(BF16)
+            for start, stop in cuts(half):
+                reward = jnp.where(
+                    first,
+                    acc1[wide + start : wide + stop, :],
+                    acc1[wide + half + start : wide + half + stop, :],
+                )
+                target[s.reward_at + start : s.reward_at + stop, :] = reward.astype(BF16)
+            here = jnp.where(first, small, 0.0)
+            target[s.small_at : s.small_at + s.held, :] = here.astype(BF16)
+            here = jnp.where(first, cond_sum[...], 0.0)
+            target[s.cond_at : s.shared_end, :] = here.astype(BF16)
+            kept = sums[...]
             for block in range(blocks):
-                gain = gain_sum[which, block : block + 1, :]
-                sums = jnp.where(lines == s.gain_row + block, gain, sums)
-            target[s.sums_at : s.reward_at, :] = sums.astype(BF16)
-            here = jnp.where(which == 0, cond_sum[...], 0.0)
-            target[s.cond_at : s.shared_end, :] = here.astype(BF16)
+                gain = gain_sum[which, block : block + 1, 0:LANES]
+                kept = jnp.where(lines == s.gain_row + block, gain, kept)
+            target[s.sums_at : s.reward_at, 0:LANES] = kept.astype(BF16)
+            kept = jnp.zeros_like(kept)
+            for block in range(blocks):
+                gain = gain_sum[which, block : block + 1, LANES:]
+                kept = jnp.where(lines == s.gain_row + block, gain, kept)
+            target[s.sums_at : s.reward_at, LANES:] = kept.astype(BF16)
             if s.total > s.shared_end:
                 target[s.shared_end :, :] = jnp.zeros((s.total - s.shared_end, width), BF16)
 
@@ -722,41 +765,40 @@
     per_pair = lambda *tail: pl.BlockSpec(
         (pair,) + tail, lambda turn, tower: (turn,) + (0,) * len(tail)
     )
-    forward_params = pltpu.CompilerParams(vmem_limit_bytes=FORWARD_LIMIT)
-    backward_params = pltpu.CompilerParams(vmem_limit_bytes=BACKWARD_LIMIT)
+    unroll_params = pltpu.CompilerParams(vmem_limit_bytes=UNROLL_LIMIT)
     small_params = pltpu.CompilerParams(vmem_limit_bytes=SMALL_LIMIT)
     products = steps * rows * (4 * blocks * width * width + 9 * width * wide)
     cost = pl.CostEstimate(flops=2 * products, bytes_accessed=40 * 2**20, transcendentals=0)
-    (
-        lat, lat_own, lat_away, entry, after, slope, side, dlat, dlast, loss, head_grads,
-        turned, code_rows, gains,
-    ) = pl.pallas_call(
-        functools.partial(forward_kernel, s),
+    turns = steps // pair
+    paired = pl.BlockSpec(
+        (pair, rows, width), lambda turn, tower: (jnp.minimum(turn, turns - 1), 0, 0)
+    )
+    lat_own, lat_away, loss, own, away, root_own, root_away = pl.pallas_call(
+        functools.partial(unroll_kernel, s),
         grid_spec=pltpu.PrefetchScalarGridSpec(
             num_scalar_prefetch=1,
-            grid=(steps // pair,),
+            grid=(2 * turns,),
             in_specs=[pl.BlockSpec(memory_space=pltpu.HBM)] * 14
             + [pl.BlockSpec(memory_space=pl.ANY)] * 4
             + [whole((blocks, width))],
             out_specs=[
-                per_pair(2, rows, width),
-                per_pair(rows, width),
-                per_pair(rows, width),
-                per_pair(calls, rows, width),
-                per_pair(calls, rows, width),
-                per_pair(calls, rows, width),
-                per_pair(calls + 2, rows, LANES),
-                pl.BlockSpec(
-                    (pair, 2, rows, width), lambda turn, tower: (jnp.maximum(turn - 1, 0), 0, 0, 0)
-                ),
-                whole((pair, 2, rows, width)),
+                paired,
+                paired,
                 whole((8, rows)),
-                whole((2, s.head_rows, width)),
-                whole((2 * calls, width, width)),
-                whole((2, steps, rows)),
-                whole((2, 8, width)),
+                whole((s.total, width)),
+                whole((s.total, width)),
+                whole((rows, half)),
+                whole((rows, half)),
             ],
             scratch_shapes=[
+                pltpu.VMEM((steps, 2, rows, width), BF16),
+                pltpu.VMEM((steps, calls, rows, width), BF16),
+                pltpu.VMEM((steps, calls, rows, width), BF16),
+                pltpu.VMEM((steps, calls, rows, width), F32),
+                pltpu.VMEM((steps, calls + 2, rows, LANES), F32),
+                pltpu.VMEM((steps, 2, rows, width), F32),
+                pltpu.VMEM((2 * calls, width, width), BF16),
+                pltpu.VMEM((2, 16, width), F32),
                 pltpu.VMEM((rows, half), BF16),
                 pltpu.VMEM((rows, half), BF16),
                 pltpu.VMEM((1, rows), jnp.int32),
@@ -787,27 +829,28 @@
                 pltpu.VMEM((s.depth[1], pair * rows), BF16),
                 pltpu.VMEM((s.reward_at - s.sums_at, LANES), F32),
                 pltpu.VMEM((pair, s.reward_at - s.sums_at, width), F32),
+                pltpu.VMEM((rows, width), F32),
+                pltpu.VMEM((2, 16, width), F32),
+                pltpu.VMEM((s.held, width), F32),
+                pltpu.VMEM((2, calls, width, width), F32),
+                pltpu.VMEM((2, 16, width), F32),
+                pltpu.VMEM((pair, calls, rows, width), BF16),
+                pltpu.VMEM((pair, calls, rows, width), BF16),
+                pltpu.VMEM((pair, 2, rows, width), BF16),
             ],
         ),
         out_shape=[
-            shape((steps, 2, rows, width), BF16),
             pltpu.HBM((steps, rows, width), BF16),
             pltpu.HBM((steps, rows, width), BF16),
-            shape((steps, calls, rows, width), BF16),
-            shape((steps, calls, rows, width), BF16),
-            shape((steps, calls, rows, width), F32),
-            shape((steps, calls + 2, rows, LANES), F32),
-            shape((steps - pair, 2, rows, width), F32),
-            shape((pair, 2, rows, width), F32),
             shape((8, rows), F32),
-            shape((2, s.head_rows, width), BF16),
-            shape((2 * calls, width, width), BF16),
-            shape((2, steps, rows), jnp.int32),
-            shape((2, 8, width), F32),
+            shape((s.total, width), BF16),
+            shape((s.total, width), BF16),
+            shape((rows, half), BF16),
+            shape((rows, half), BF16),
         ],
-        compiler_params=forward_params,
+        compiler_params=unroll_params,
         cost_estimate=cost,
-        name="unroll_forward",
+        name="unroll",
     )(
         tower_ref,
         *[
@@ -819,63 +862,6 @@
             )
         ],
         root_got, in_got, out_got, value_got, gains_got,
-    )
-
-    turns = steps // pair
-    descending = lambda *tail: pl.BlockSpec(
-        (pair,) + tail, lambda turn, tower: (turns - 1 - turn,) + (0,) * len(tail)
-    )
-    own, away, root_own, root_away = pl.pallas_call(
-        functools.partial(backward_kernel, s),
-        grid_spec=pltpu.PrefetchScalarGridSpec(
-            num_scalar_prefetch=1,
-            grid=(turns,),
-            in_specs=[
-                descending(2, rows, width),
-                descending(calls, rows, width),
-                descending(calls, rows, width),
-                descending(calls, rows, width),
-                descending(calls + 2, rows, LANES),
-                pl.BlockSpec(
-                    (pair, 2, rows, width),
-                    lambda turn, tower: (jnp.minimum(turns - 1 - turn, turns - 2), 0, 0, 0),
-                ),
-                whole((pair, 2, rows, width)),
-                whole((2, steps, rows)),
-                whole((2, 8, width)),
-                whole((2 * calls, width, width)),
-                whole((2, s.head_rows, width)),
-            ],
-            out_specs=[
-                whole((s.total, width)),
-                whole((s.total, width)),
-                whole((rows, half)),
-                whole((rows, half)),
-            ],
-            scratch_shapes=[
-                pltpu.VMEM((rows, width), F32),
-                pltpu.VMEM((2, 16, width), F32),
-                pltpu.VMEM((s.held, width), F32),
-                pltpu.VMEM((2, calls, width, width), F32),
-                pltpu.VMEM((2, 16, width), F32),
-                pltpu.VMEM((2, 16, width), F32),
-                pltpu.VMEM((pair, calls, rows, width), BF16),
-                pltpu.VMEM((pair, calls, rows, width), BF16),
-                pltpu.VMEM((pair, 2, rows, width), BF16),
-            ],
-        ),
-        out_shape=[
-            shape((s.total, width), BF16),
-            shape((s.total, width), BF16),
-            shape((rows, half), BF16),
-            shape((rows, half), BF16),
-        ],
-        compiler_params=backward_params,
-        cost_estimate=cost,
-        name="unroll_backward",
-    )(
-        tower_ref, lat, entry, after, slope, side, dlat, dlast, code_rows, gains,
-        turned, head_grads,
     )
     got = swap(away, "tower", 1)
 

time: 111 us -> 110 us (level)
  Pallas kernels: 60.4 us -> 59.1 us
    pallas_call x2 -> x1, Pallas kernels: 50.1 us -> 48.8 us  [body(): pl.pallas_call(functools.partial(unroll_kernel, s), grid_spec=pltpu.Prefe...]
where the time goes in v1:
time: 110 us; the launch traced here: 109 us
  Pallas kernels  59.1 us (54%)
  waiting for transfers between devices  35.4 us (32%)
  starting transfers between devices  11.9 us (11%)
  other arithmetic  1.36 us (1%)
    pallas_call x1, Pallas kernels, body(): pl.pallas_call(functools.partial(unroll_kernel, s), grid_spec=pltpu.Prefe...  48.8 us
    ppermute x8, waiting for transfers between devices, swap_within(): return lax.ppermute(value, AXES, pairs)  29.7 us
    ppermute x8, starting transfers between devices, swap_within(): return lax.ppermute(value, AXES, pairs)  7.94 us
    pallas_call x1, Pallas kernels, beside(): pl.pallas_call(functools.partial(logits_kernel, s), grid_spec=pltpu.Prefe...  5.73 us
    ppermute x10, waiting for transfers between devices, swap(): return lax.ppermute(value, axis, pairs)  5.69 us
    ppermute x10, starting transfers between devices, swap(): return lax.ppermute(value, axis, pairs)  3.92 us
  transfers between devices with their start and end apart: 18, of which 11 were waited for; matrix products, arithmetic and copies ran while one was open for 1% of the time, Pallas kernels for 7%

profile of v1, /device:TPU:9, one launch (start us, length us, event | category | flops | bytes accessed | tf_op | source)
XLA Modules:
  0.0 109.3 jit_solution(14516290917607290280)
XLA Ops:
  0.6 0.7 collective-permute-start.1
  1.4 0.1 collective-permute-start.2
  1.5 0.4 collective-permute-start.3
  1.9 0.1 collective-permute-start
  2.0 0.4 collective-permute-start.4
  2.4 1.6 %collective-permute-done.4.gains_got = bf16[3,256]{1,0:T(4,128)(2,1)S(1)} collective-permute-done((bf16[3,256]{1,0:T(4,128)(2,1)}, bf16[3,256]{1,0:T(4,128)(2,1)S(1)}, u32[]{:S(2)}, u32[]{:S(2)}) %collective-permute-start.4) | collective-permute-done | bytes 1568 | tf_op jit(solution)/shard_map/ppermute | solution.py:653
  4.1 0.0 collective-permute-done.root_any
  4.1 0.0 collective-permute-done.3.value_any
  4.1 0.0 collective-permute-done.1.in_got
  4.1 0.0 collective-permute-done.2.out_got
  4.1 48.8 %unroll.1 = (bf16[10,128,256]{2,1,0:T(8,128)(2,1)}, bf16[10,128,256]{2,1,0:T(8,128)(2,1)}, f32[8,128]{1,0:T(8,128)S(1)}, bf16[2560,256]{1,0:T(8,128)(2,1)S(1)}, ...) custom-call(s32[1]{0:T(128)} %bitcast.1.tower_ref, ...), custom_call_target="tpu_custom_call" | custom-call | flops 5599395840 | bytes 41943040 | tf_op jit(solution)/shard_map/unroll/pallas_call | solution.py:776
  52.9 0.4 collective-permute-start.5
  53.3 2.9 %collective-permute-done.5 = bf16[2560,256]{1,0:T(8,128)(2,1)S(1)} collective-permute-done((bf16[2560,256]{1,0:T(8,128)(2,1)}, bf16[2560,256]{1,0:T(8,128)(2,1)S(1)}, u32[]{:S(2)}, u32[]{:S(2)}) %collective-permute-start.5) | collective-permute-done | bytes 1310752 | tf_op jit(solution)/shard_map/ppermute | solution.py:653
  56.2 1.3 %add_and_split.1 = (bf16[640,256]{1,0:T(8,128)(2,1)}, bf16[640,256]{1,0:T(8,128)(2,1)}, bf16[640,256]{1,0:T(8,128)(2,1)}, bf16[640,256]{1,0:T(8,128)(2,1)}) custom-call(s32[1]{0:T(128)} %bitcast.digit_ref, bf16[4,640,256]{2,1,0:T(8,128)(2,1)S(1)} %bitcast.29, bf16[4,640,256]{2,1,0:T(8,128)(2,1)S(1)} %bitcast.30), custom_call_target="tpu_custom_call" | custom-call | tf_op jit(solution)/shard_map/add_and_split/pallas_call | solution.py:707
  57.5 0.4 collective-permute-start.9
  57.9 0.0 collective-permute-start.6
  57.9 2.5 %collective-permute-start.7 = (bf16[640,256]{1,0:T(8,128)(2,1)}, bf16[640,256]{1,0:T(8,128)(2,1)S(1)}, u32[]{:S(2)}, u32[]{:S(2)}) collective-permute-start(bf16[640,256]{1,0:T(8,128)(2,1)} %get-tuple-element.63), channel_id=1, source_target_pairs={{0,2},{1,3},{2,0},{3,1},{4,6},{5,7},{6,4},{7,5},{8,10},{9,11},{10,... | collective-permute-start | bytes 983048 | tf_op jit(solution)/shard_map/ppermute | solution.py:678
  60.3 0.2 collective-permute-start.8
  60.5 1.0 collective-permute-start.10
  61.5 0.8 collective-permute-done.10
  62.3 0.3 collective-permute-start.11
  62.6 0.6 maximum_select_fusion.1
  63.2 0.3 collective-permute-done.11
  63.5 0.7 fusion.2
  64.2 0.0 collective-permute-done.9.lat_got
  64.2 0.8 copy-done.2
  65.0 5.7 %latents_and_logits.1 = (bf16[10,256,256]{2,1,0:T(8,128)(2,1)}, bf16[10,601,256]{2,1,0:T(8,128)(2,1)}) custom-call(s32[1]{0:T(128)} %bitcast.1.tower_ref, bf16[10,128,256]{2,1,0:T(8,128)(2,1)} %get-tuple-element.65.lat_own, bf16[10,128,256]{2,1,0:T(8,128)(2,1)} %copy-done.2, bf16[601,256]{1,0:T(8,128)(2,1)} %bitcast.42), custom_call_target="tpu_custom_call" | custom-call | flops 796917760 | bytes 6291456 | tf_op jit(solution)/shard_map/latents_and_logits/pallas_call | solution.py:875
  70.8 0.0 collective-permute-done.6.refs_1_
  70.8 1.0 collective-permute-done.7.refs_2_
  71.7 4.3 %collective-permute-done.8.refs_3_ = bf16[640,256]{1,0:T(8,128)(2,1)S(1)} collective-permute-done((bf16[640,256]{1,0:T(8,128)(2,1)}, bf16[640,256]{1,0:T(8,128)(2,1)S(1)}, u32[]{:S(2)}, u32[]{:S(2)}) %collective-permute-start.8) | collective-permute-done | bytes 327712 | tf_op jit(solution)/shard_map/ppermute | solution.py:678
  76.1 0.2 add_up.3.refs_0_
  76.2 1.3 %collective-permute-start.12 = (bf16[640,256]{1,0:T(8,128)(2,1)S(1)}, bf16[640,256]{1,0:T(8,128)(2,1)S(1)}, u32[]{:S(2)}, u32[]{:S(2)}) collective-permute-start(bf16[640,256]{1,0:T(8,128)(2,1)S(1)} %add_up.3.refs_0_), channel_id=1, source_target_pairs={{0,4},{1,5},{2,6},{3,7},{4,0},{5,1},{6,2},{7,3},{8,12},{9,13},{10,... | collective-permute-start | bytes 983048 | tf_op jit(solution)/shard_map/ppermute | solution.py:678
  77.5 4.7 %collective-permute-done.12.refs_1_ = bf16[640,256]{1,0:T(8,128)(2,1)S(1)} collective-permute-done((bf16[640,256]{1,0:T(8,128)(2,1)S(1)}, bf16[640,256]{1,0:T(8,128)(2,1)S(1)}, u32[]{:S(2)}, u32[]{:S(2)}) %collective-permute-start.12) | collective-permute-done | bytes 327712 | tf_op jit(solution)/shard_map/ppermute | solution.py:678
  82.2 0.1 add_up.4.refs_0_
  82.3 1.3 %collective-permute-start.13 = (bf16[640,256]{1,0:T(8,128)(2,1)S(1)}, bf16[640,256]{1,0:T(8,128)(2,1)S(1)}, u32[]{:S(2)}, u32[]{:S(2)}) collective-permute-start(bf16[640,256]{1,0:T(8,128)(2,1)S(1)} %add_up.4.refs_0_), channel_id=1, source_target_pairs={{0,8},{1,9},{2,10},{3,11},{4,12},{5,13},{6,14},{7,15},{8,0},{9,1},... | collective-permute-start | bytes 983048 | tf_op jit(solution)/shard_map/ppermute | solution.py:678
  83.6 4.7 %collective-permute-done.13.refs_1_ = bf16[640,256]{1,0:T(8,128)(2,1)S(1)} collective-permute-done((bf16[640,256]{1,0:T(8,128)(2,1)S(1)}, bf16[640,256]{1,0:T(8,128)(2,1)S(1)}, u32[]{:S(2)}, u32[]{:S(2)}) %collective-permute-start.13) | collective-permute-done | bytes 327712 | tf_op jit(solution)/shard_map/ppermute | solution.py:678
  88.3 0.1 add_up.5.refs_0_
  88.4 0.1 collective-permute-start.14
  88.5 2.5 %collective-permute-start.15 = (bf16[640,256]{1,0:T(8,128)(2,1)S(1)}, bf16[640,256]{1,0:T(8,128)(2,1)S(1)}, u32[]{:S(2)}, u32[]{:S(2)}) collective-permute-start(bf16[640,256]{1,0:T(8,128)(2,1)S(1)} %add_up.5.refs_0_), channel_id=1, source_target_pairs={{0,2},{1,3},{2,0},{3,1},{4,6},{5,7},{6,4},{7,5},{8,10},{9,11},{10,... | collective-permute-start | bytes 983048 | tf_op jit(solution)/shard_map/ppermute | solution.py:678
  90.9 0.2 collective-permute-start.16
  91.1 4.8 %collective-permute-done.14.refs_1_ = bf16[640,256]{1,0:T(8,128)(2,1)S(1)} collective-permute-done((bf16[640,256]{1,0:T(8,128)(2,1)S(1)}, bf16[640,256]{1,0:T(8,128)(2,1)S(1)}, u32[]{:S(2)}, u32[]{:S(2)}) %collective-permute-start.14) | collective-permute-done | bytes 327712 | tf_op jit(solution)/shard_map/ppermute | solution.py:678
  95.9 6.1 %collective-permute-done.15.refs_2_ = bf16[640,256]{1,0:T(8,128)(2,1)S(1)} collective-permute-done((bf16[640,256]{1,0:T(8,128)(2,1)S(1)}, bf16[640,256]{1,0:T(8,128)(2,1)S(1)}, u32[]{:S(2)}, u32[]{:S(2)}) %collective-permute-start.15) | collective-permute-done | bytes 327712 | tf_op jit(solution)/shard_map/ppermute | solution.py:678
  102.0 4.1 %collective-permute-done.16.refs_3_ = bf16[640,256]{1,0:T(8,128)(2,1)S(1)} collective-permute-done((bf16[640,256]{1,0:T(8,128)(2,1)S(1)}, bf16[640,256]{1,0:T(8,128)(2,1)S(1)}, u32[]{:S(2)}, u32[]{:S(2)}) %collective-permute-start.16) | collective-permute-done | bytes 327712 | tf_op jit(solution)/shard_map/ppermute | solution.py:678
  106.2 0.1 collective-permute-start.17
  106.3 0.1 pad_add_fusion.scalars
  106.3 2.0 %unpack_own.1 = (f32[3,256,256]{2,1,0:T(8,128)}, f32[3,256,256]{2,1,0:T(8,128)}, f32[601,1,256]{2,1,0:T(1,128)}, f32[3,1,256]{2,1,0:T(1,128)}, f32[3,2,10]{2,1,0:T(2,128)}) custom-call(s32[2]{0:T(128)S(1)} %pad_add_fusion.scalars, bf16[640,256]{1,0:T(8,128)(2,1)S(1)} %add_up.5.refs_0_, bf16[640,256]{1,0:T(8,128)(2,1)S(1)} %collective-permute-done.14.refs_1_, ...), custom_call_target="tpu_custom_call" | custom-call | tf_op jit(solution)/shard_map/unpack_own/pallas_call | solution.py:923
  108.4 0.0 collective-permute-done.17.got
  108.4 0.9 unpack_shared.1
  (7 shorter events, 0.1 us)
Async XLA Ops:
  0.6 3.4 %collective-permute-start.1 = (bf16[3,256,256]{2,1,0:T(8,128)(2,1)}, bf16[3,256,256]{2,1,0:T(8,128)(2,1)S(1)}, u32[]{:S(2)}, u32[]{:S(2)}) collective-permute-start(bf16[3,256,256]{2,1,0:T(8,128)(2,1)} %bitcast.35), channel_id=1, source_target_pairs={{0,16},{16,0},{1,17},{17,1},{2,18},{18,2},{3,19},{19,3},{4,20},{20... | collective-permute-start | bytes 1179656 | tf_op jit(solution)/shard_map/ppermute | solution.py:653
  1.4 2.7 %collective-permute-start.2 = (bf16[3,256,256]{2,1,0:T(8,128)(2,1)}, bf16[3,256,256]{2,1,0:T(8,128)(2,1)S(1)}, u32[]{:S(2)}, u32[]{:S(2)}) collective-permute-start(bf16[3,256,256]{2,1,0:T(8,128)(2,1)} %bitcast.37), channel_id=1, source_target_pairs={{0,16},{16,0},{1,17},{17,1},{2,18},{18,2},{3,19},{19,3},{4,20},{20... | collective-permute-start | bytes 1179656 | tf_op jit(solution)/shard_map/ppermute | solution.py:653
  1.5 2.6 %collective-permute-start.3 = (bf16[601,256]{1,0:T(8,128)(2,1)}, bf16[601,256]{1,0:T(8,128)(2,1)S(1)}, u32[]{:S(2)}, u32[]{:S(2)}) collective-permute-start(bf16[601,256]{1,0:T(8,128)(2,1)} %bitcast.40), channel_id=1, source_target_pairs={{0,16},{16,0},{1,17},{17,1},{2,18},{18,2},{3,19},{19,3},{4,20},{20... | collective-permute-start | bytes 923144 | tf_op jit(solution)/shard_map/ppermute | solution.py:653
  1.9 2.2 %collective-permute-start = (bf16[256,128]{1,0:T(8,128)(2,1)}, bf16[256,128]{1,0:T(8,128)(2,1)S(1)}, u32[]{:S(2)}, u32[]{:S(2)}) collective-permute-start(bf16[256,128]{1,0:T(8,128)(2,1)} %root_hbm.1), channel_id=1, source_target_pairs={{0,16},{16,0},{1,17},{17,1},{2,18},{18,2},{3,19},{19,3},{4,20},{20... | collective-permute-start | bytes 196616 | tf_op jit(solution)/shard_map/ppermute | solution.py:653
  2.0 2.1 %collective-permute-start.4 = (bf16[3,256]{1,0:T(4,128)(2,1)}, bf16[3,256]{1,0:T(4,128)(2,1)S(1)}, u32[]{:S(2)}, u32[]{:S(2)}) collective-permute-start(bf16[3,256]{1,0:T(4,128)(2,1)} %bitcast.48), channel_id=1, source_target_pairs={{0,16},{16,0},{1,17},{17,1},{2,18},{18,2},{3,19},{19,3},{4,20},{20... | collective-permute-start | bytes 4616 | tf_op jit(solution)/shard_map/ppermute | solution.py:653
  52.9 3.3 %collective-permute-start.5 = (bf16[2560,256]{1,0:T(8,128)(2,1)}, bf16[2560,256]{1,0:T(8,128)(2,1)S(1)}, u32[]{:S(2)}, u32[]{:S(2)}) collective-permute-start(bf16[2560,256]{1,0:T(8,128)(2,1)} %get-tuple-element.51), channel_id=1, source_target_pairs={{0,16},{16,0},{1,17},{17,1},{2,18},{18,2},{3,19},{19,3},{4,20},{20... | collective-permute-start | bytes 3932168 | tf_op jit(solution)/shard_map/ppermute | solution.py:653
  56.2 1.3 %copy-start.1 = (bf16[10,128,256]{2,1,0:T(8,128)(2,1)S(1)}, bf16[10,128,256]{2,1,0:T(8,128)(2,1)}, u32[]{:S(2)}) copy-start(bf16[10,128,256]{2,1,0:T(8,128)(2,1)} %get-tuple-element.66) | copy-start | bytes 1966084
  57.5 6.7 %collective-permute-start.9 = (bf16[10,128,256]{2,1,0:T(8,128)(2,1)S(1)}, bf16[10,128,256]{2,1,0:T(8,128)(2,1)S(1)}, u32[]{:S(2)}, u32[]{:S(2)}) collective-permute-start(bf16[10,128,256]{2,1,0:T(8,128)(2,1)S(1)} %copy-done.1), channel_id=1, source_target_pairs={{0,16},{16,0},{1,17},{17,1},{2,18},{18,2},{3,19},{19,3},{4,20},{20... | collective-permute-start | bytes 1966088 | tf_op jit(solution)/shard_map/ppermute | solution.py:653
  57.9 12.9 %collective-permute-start.6 = (bf16[640,256]{1,0:T(8,128)(2,1)}, bf16[640,256]{1,0:T(8,128)(2,1)S(1)}, u32[]{:S(2)}, u32[]{:S(2)}) collective-permute-start(bf16[640,256]{1,0:T(8,128)(2,1)} %get-tuple-element.62), channel_id=1, source_target_pairs={{0,1},{1,0},{2,3},{3,2},{4,5},{5,4},{6,7},{7,6},{8,9},{9,8},{10,11... | collective-permute-start | bytes 983048 | tf_op jit(solution)/shard_map/ppermute | solution.py:678
  57.9 13.9 %collective-permute-start.7 = (bf16[640,256]{1,0:T(8,128)(2,1)}, bf16[640,256]{1,0:T(8,128)(2,1)S(1)}, u32[]{:S(2)}, u32[]{:S(2)}) collective-permute-start(bf16[640,256]{1,0:T(8,128)(2,1)} %get-tuple-element.63), channel_id=1, source_target_pairs={{0,2},{1,3},{2,0},{3,1},{4,6},{5,7},{6,4},{7,5},{8,10},{9,11},{10,... | collective-permute-start | bytes 983048 | tf_op jit(solution)/shard_map/ppermute | solution.py:678
  60.3 15.7 %collective-permute-start.8 = (bf16[640,256]{1,0:T(8,128)(2,1)}, bf16[640,256]{1,0:T(8,128)(2,1)S(1)}, u32[]{:S(2)}, u32[]{:S(2)}) collective-permute-start(bf16[640,256]{1,0:T(8,128)(2,1)} %get-tuple-element.64), channel_id=1, source_target_pairs={{0,3},{1,2},{2,1},{3,0},{4,7},{5,6},{6,5},{7,4},{8,11},{9,10},{10,... | collective-permute-start | bytes 983048 | tf_op jit(solution)/shard_map/ppermute | solution.py:678
  60.5 1.8 %collective-permute-start.10 = (f32[128]{0:T(128)S(1)}, f32[128]{0:T(128)S(1)}, u32[]{:S(2)}, u32[]{:S(2)}) collective-permute-start(f32[128]{0:T(128)S(1)} %slice_bitcast_fusion), channel_id=1, source_target_pairs={{0,16},{16,0},{1,17},{17,1},{2,18},{18,2},{3,19},{19,3},{4,20},{20... | collective-permute-start | bytes 1544 | tf_op jit(solution)/shard_map/ppermute | solution.py:653
  62.3 1.2 %collective-permute-start.11 = (bf16[128,128]{1,0:T(8,128)(2,1)S(1)}, bf16[128,128]{1,0:T(8,128)(2,1)S(1)}, u32[]{:S(2)}, u32[]{:S(2)}) collective-permute-start(bf16[128,128]{1,0:T(8,128)(2,1)S(1)} %get-tuple-element.71), channel_id=1, source_target_pairs={{0,16},{16,0},{1,17},{17,1},{2,18},{18,2},{3,19},{19,3},{4,20},{20... | collective-permute-start | bytes 98312 | tf_op jit(solution)/shard_map/ppermute | solution.py:653
  64.2 11.9 %copy-start = (bf16[640,256]{1,0:T(8,128)(2,1)S(1)}, bf16[640,256]{1,0:T(8,128)(2,1)}, u32[]{:S(2)}) copy-start(bf16[640,256]{1,0:T(8,128)(2,1)} %get-tuple-element.75.refs_0_) | copy-start | bytes 983044
  64.2 0.8 copy-start.2
  76.2 6.0 %collective-permute-start.12 = (bf16[640,256]{1,0:T(8,128)(2,1)S(1)}, bf16[640,256]{1,0:T(8,128)(2,1)S(1)}, u32[]{:S(2)}, u32[]{:S(2)}) collective-permute-start(bf16[640,256]{1,0:T(8,128)(2,1)S(1)} %add_up.3.refs_0_), channel_id=1, source_target_pairs={{0,4},{1,5},{2,6},{3,7},{4,0},{5,1},{6,2},{7,3},{8,12},{9,13},{10,... | collective-permute-start | bytes 983048 | tf_op jit(solution)/shard_map/ppermute | solution.py:678
  82.3 6.0 %collective-permute-start.13 = (bf16[640,256]{1,0:T(8,128)(2,1)S(1)}, bf16[640,256]{1,0:T(8,128)(2,1)S(1)}, u32[]{:S(2)}, u32[]{:S(2)}) collective-permute-start(bf16[640,256]{1,0:T(8,128)(2,1)S(1)} %add_up.4.refs_0_), channel_id=1, source_target_pairs={{0,8},{1,9},{2,10},{3,11},{4,12},{5,13},{6,14},{7,15},{8,0},{9,1},... | collective-permute-start | bytes 983048 | tf_op jit(solution)/shard_map/ppermute | solution.py:678
  88.4 7.5 %collective-permute-start.14 = (bf16[640,256]{1,0:T(8,128)(2,1)S(1)}, bf16[640,256]{1,0:T(8,128)(2,1)S(1)}, u32[]{:S(2)}, u32[]{:S(2)}) collective-permute-start(bf16[640,256]{1,0:T(8,128)(2,1)S(1)} %add_up.5.refs_0_), channel_id=1, source_target_pairs={{0,1},{1,0},{2,3},{3,2},{4,5},{5,4},{6,7},{7,6},{8,9},{9,8},{10,11... | collective-permute-start | bytes 983048 | tf_op jit(solution)/shard_map/ppermute | solution.py:678
  88.5 13.6 %collective-permute-start.15 = (bf16[640,256]{1,0:T(8,128)(2,1)S(1)}, bf16[640,256]{1,0:T(8,128)(2,1)S(1)}, u32[]{:S(2)}, u32[]{:S(2)}) collective-permute-start(bf16[640,256]{1,0:T(8,128)(2,1)S(1)} %add_up.5.refs_0_), channel_id=1, source_target_pairs={{0,2},{1,3},{2,0},{3,1},{4,6},{5,7},{6,4},{7,5},{8,10},{9,11},{10,... | collective-permute-start | bytes 983048 | tf_op jit(solution)/shard_map/ppermute | solution.py:678
  90.9 15.2 %collective-permute-start.16 = (bf16[640,256]{1,0:T(8,128)(2,1)S(1)}, bf16[640,256]{1,0:T(8,128)(2,1)S(1)}, u32[]{:S(2)}, u32[]{:S(2)}) collective-permute-start(bf16[640,256]{1,0:T(8,128)(2,1)S(1)} %add_up.5.refs_0_), channel_id=1, source_target_pairs={{0,3},{1,2},{2,1},{3,0},{4,7},{5,6},{6,5},{7,4},{8,11},{9,10},{10,... | collective-permute-start | bytes 983048 | tf_op jit(solution)/shard_map/ppermute | solution.py:678
  106.2 2.2 %collective-permute-start.17 = (bf16[400,256]{1,0:T(8,128)(2,1)S(1)}, bf16[400,256]{1,0:T(8,128)(2,1)S(1)}, u32[]{:S(2)}, u32[]{:S(2)}) collective-permute-start(bf16[400,256]{1,0:T(8,128)(2,1)S(1)} %fusion.1.mine), channel_id=1, source_target_pairs={{0,16},{16,0},{1,17},{17,1},{2,18},{18,2},{3,19},{19,3},{4,20},{20... | collective-permute-start | bytes 614408 | tf_op jit(solution)/shard_map/ppermute | solution.py:653

commit v2 on v1

--- a/solution.py
+++ b/solution.py
@@ -10,7 +10,7 @@
 ACTIONS = 4
 LANES = 128
 MIB = 1024 * 1024
-UNROLL_LIMIT = 46 * MIB
+UNROLL_LIMIT = 58 * MIB
 SMALL_LIMIT = 12 * MIB
 epsilon = 1e-06
 very_negative = -1e30
@@ -94,11 +94,8 @@
     logits0, logits1, cot0, cot1, sums, squares,
     carry, gain_sum, cond_sum, grads, inverse_gains, d_after_kept, d_before_kept, d_hidden_kept,
 ):
-    turn = pl.program_id(0)
     turns = sizes.steps // sizes.pair
-
-    @pl.when(turn < turns)
-    def _():
+    for turn in range(turns):
         forward_turn(
             sizes, turn, tower_ref,
             root_hbm, lengths_hbm, actions_hbm, codes_hbm, policy_hbm, value_bins_hbm,
@@ -110,11 +107,9 @@
             state, past0, past1, table, weights, heads0, heads1, acc0, acc1,
             logits0, logits1, cot0, cot1, sums, squares,
         )
-
-    @pl.when(turn >= turns)
-    def _():
+    for turn in range(turns):
         backward_turn(
-            sizes, turn - turns, tower_ref,
+            sizes, turn, tower_ref,
             lat, entry, after, slope, side, dlat, actions, codes, turned, acc0, acc1, sums,
             own, away, root_own_grad, root_away_grad,
             carry, gain_sum, cond_sum, grads, gains, inverse_gains, d_after_kept, d_before_kept,
@@ -139,8 +134,7 @@
     tower_id = tower_ref[0]
     rows, width, wide = s.rows, s.width, s.wide
 
-    @pl.when(turn == 0)
-    def _():
+    if turn == 0:
         here = pl.ds(pl.multiple_of(tower_id * rows, rows), rows)
 
         def matrices(kind, tower):
@@ -192,11 +186,12 @@
         heads1[2 * wide : 2 * wide + s.table_rows, :] = small_in[...]
 
     eights = lax.broadcasted_iota(jnp.int32, (8, pair * rows), 0)
-    before = jnp.maximum(first_step - pair, 0)
+    before = first_step - pair
 
     def pair_row(kind, at_step, lead=()):
         return jnp.concatenate(
-            [kind[(pl.ds(at_step + offset, 1),) + lead] for offset in range(pair)], axis=1
+            [kind[(slice(at_step + offset, at_step + offset + 1),) + lead] for offset in range(pair)],
+            axis=1,
         )
 
     def live_rows(at_step):
@@ -208,8 +203,8 @@
     for offset in range(pair):
         step = first_step + offset
         kinds.append((step < lengths[...]).astype(F32))
-        kinds.append(actions[pl.ds(step, 1), :].astype(F32))
-        kinds.append((codes[pl.ds(step, 1), :] + ACTIONS).astype(F32))
+        kinds.append(actions[step : step + 1, :].astype(F32))
+        kinds.append((codes[step : step + 1, :] + ACTIONS).astype(F32))
     kinds.append(jnp.zeros((8 - len(kinds), rows), F32))
     columns = jnp.concatenate(kinds, axis=0).T
 
@@ -315,7 +310,7 @@
         def keep_squares(block, row_squares):
             place = 2 * (tower * s.blocks + block)
             total = jnp.sum(live * row_squares, axis=0, keepdims=True) * (1.0 / LANES)
-            squares[offset, place : place + 1, 0:LANES] = jnp.broadcast_to(total, (1, LANES))
+            squares[first_step + offset, place : place + 1, 0:LANES] = jnp.broadcast_to(total, (1, LANES))
 
         def end_block(block):
             branch = chain["product"]
@@ -324,7 +319,7 @@
 
         def keep_branch(block, branch):
             spot = 2 * (tower * s.blocks + block) + 1
-            squares[offset, spot : spot + 1, :] = jnp.sum(
+            squares[first_step + offset, spot : spot + 1, :] = jnp.sum(
                 branch * branch * live, axis=0, keepdims=True
             )
 
@@ -349,7 +344,7 @@
             after_rows = (u * gate).astype(BF16)
             chain["product"] = natural(after_rows, weights[s.calls + place])
             after[first_step + offset, place] = after_rows
-            slope[first_step + offset, place] = gate * (1.0 + u * (1.0 - gate))
+            slope[first_step + offset, place] = (gate * (1.0 + u * (1.0 - gate))).astype(BF16)
 
         def finish():
             branch = end_block(s.blocks - 1)
@@ -367,7 +362,7 @@
                 keep_branch(s.blocks - 1, branch)
                 if tower == 0:
                     total = jnp.sum(live, axis=0, keepdims=True) * (1.0 / LANES)
-                    squares[offset, s.kinds : s.kinds + 1, 0:LANES] = jnp.broadcast_to(
+                    squares[first_step + offset, s.kinds : s.kinds + 1, 0:LANES] = jnp.broadcast_to(
                         total, (1, LANES)
                     )
 
@@ -402,17 +397,16 @@
 
     turns = -(-2 * s.calls // (s.steps // pair))
 
-    def turn_weights(which):
-        matrix = jnp.minimum(turn * turns + which, 2 * s.calls - 1)
+    def turn_weights(matrix):
         turned[matrix] = weights[matrix].T
 
-    live_before = jnp.where(turn > 0, live_rows(before), 0.0)
-    weave(
-        pieces,
-        heads(1, live_before, before, dlat)
-        + heads(0, live_before, before, dlat)
-        + [functools.partial(turn_weights, which) for which in range(turns)],
-    )
+    beside = []
+    if turn > 0:
+        live_before = live_rows(before)
+        beside += heads(1, live_before, before, dlat) + heads(0, live_before, before, dlat)
+    matrices_now = range(turn * turns, min((turn + 1) * turns, 2 * s.calls))
+    beside += [functools.partial(turn_weights, matrix) for matrix in matrices_now]
+    weave(pieces, beside)
     first = tower_id == 0
     at_lane = lax.broadcasted_iota(jnp.int32, sums.shape, 1)
     for offset in range(pair):
@@ -420,17 +414,17 @@
         after_state, next_state = chain[offset, 0], chain[offset, 1]
         past0[at, :] = after_state
         past1[at, :] = next_state
-        lat_own[offset] = jnp.where(first, after_state, next_state)
-        lat_away[offset] = jnp.where(first, next_state, after_state)
+        lat_own[first_step + offset] = jnp.where(first, after_state, next_state)
+        lat_away[first_step + offset] = jnp.where(first, next_state, after_state)
         if offset == pair - 1:
             state[...] = next_state
-        total = lane_sum(squares[offset])
+        total = lane_sum(squares[first_step + offset])
         sums[...] = jnp.where(at_lane == first_step + offset, total, sums[...])
 
-    @pl.when(turn == s.steps // pair - 1)
-    def _():
+    if turn == s.steps // pair - 1:
         live_now = live_rows(first_step)
-        weave(heads(1, live_now, first_step, dlat), heads(0, live_now, first_step, dlat))
+        for piece in heads(1, live_now, first_step, dlat) + heads(0, live_now, first_step, dlat):
+            piece()
 
 
 def backward_turn(
@@ -446,8 +440,7 @@
     tower_id = tower_ref[0]
     blocks, width = s.blocks, s.width
 
-    @pl.when(turn == 0)
-    def _():
+    if turn == 0:
         inverse_gains[...] = 1.0 / gains[...]
         carry[...] = jnp.zeros_like(carry)
         grads[...] = jnp.zeros_like(grads)
@@ -472,7 +465,11 @@
             return
         codes_of, shift = (actions, 0) if tower == 0 else (codes, ACTIONS)
         code = jnp.concatenate(
-            [codes_of[pl.ds(first_step + step, 1), :] + shift for step in range(pair)], axis=1
+            [
+                codes_of[first_step + step : first_step + step + 1, :] + shift
+                for step in range(pair)
+            ],
+            axis=1,
         )
         spots = lax.broadcasted_iota(jnp.int32, (cond_sum.shape[0], pair * s.rows), 0)
         onehot = jnp.where(spots == code, 1.0, 0.0).astype(BF16)
@@ -504,7 +501,7 @@
             inv_scale = over_lanes(side[first_step + offset, place])
             catch_up()
             d_after = both[s.rows :] - slant * both[: s.rows]
-            d_before = (d_after * slope[first_step + offset, place]).astype(BF16)
+            d_before = (d_after * slope[first_step + offset, place].astype(F32)).astype(BF16)
             d_entry = natural(d_before, turned[place])
             if offset > 0:
                 d_after_kept[offset, place] = d_branch
@@ -539,8 +536,7 @@
     catch_up()
     carry[...] = d_state
 
-    @pl.when(turn == s.steps // pair - 1)
-    def _():
+    if turn == s.steps // pair - 1:
         left = d_state[:, 0 : width // 2].astype(BF16)
         right = d_state[:, width // 2 : width].astype(BF16)
         root_own[...] = jnp.where(tower_id == 0, left, right)
@@ -769,21 +765,17 @@
     small_params = pltpu.CompilerParams(vmem_limit_bytes=SMALL_LIMIT)
     products = steps * rows * (4 * blocks * width * width + 9 * width * wide)
     cost = pl.CostEstimate(flops=2 * products, bytes_accessed=40 * 2**20, transcendentals=0)
-    turns = steps // pair
-    paired = pl.BlockSpec(
-        (pair, rows, width), lambda turn, tower: (jnp.minimum(turn, turns - 1), 0, 0)
-    )
     lat_own, lat_away, loss, own, away, root_own, root_away = pl.pallas_call(
         functools.partial(unroll_kernel, s),
         grid_spec=pltpu.PrefetchScalarGridSpec(
             num_scalar_prefetch=1,
-            grid=(2 * turns,),
+            grid=(1,),
             in_specs=[pl.BlockSpec(memory_space=pltpu.HBM)] * 14
             + [pl.BlockSpec(memory_space=pl.ANY)] * 4
             + [whole((blocks, width))],
             out_specs=[
-                paired,
-                paired,
+                whole((steps, rows, width)),
+                whole((steps, rows, width)),
                 whole((8, rows)),
                 whole((s.total, width)),
                 whole((s.total, width)),
@@ -794,7 +786,7 @@
                 pltpu.VMEM((steps, 2, rows, width), BF16),
                 pltpu.VMEM((steps, calls, rows, width), BF16),
                 pltpu.VMEM((steps, calls, rows, width), BF16),
-                pltpu.VMEM((steps, calls, rows, width), F32),
+                pltpu.VMEM((steps, calls, rows, width), BF16),
                 pltpu.VMEM((steps, calls + 2, rows, LANES), F32),
                 pltpu.VMEM((steps, 2, rows, width), F32),
                 pltpu.VMEM((2 * calls, width, width), BF16),
@@ -828,7 +820,7 @@
                 pltpu.VMEM((s.depth[0], pair * rows), BF16),
                 pltpu.VMEM((s.depth[1], pair * rows), BF16),
                 pltpu.VMEM((s.reward_at - s.sums_at, LANES), F32),
-                pltpu.VMEM((pair, s.reward_at - s.sums_at, width), F32),
+                pltpu.VMEM((steps, s.reward_at - s.sums_at, width), F32),
                 pltpu.VMEM((rows, width), F32),
                 pltpu.VMEM((2, 16, width), F32),
                 pltpu.VMEM((s.held, width), F32),

time: 110 us -> 107 us (0.973)
  Pallas kernels: 59.1 us -> 54.6 us
  local copies, waits for them, and re-layouts: 0.85 us -> 3.79 us
    pallas_call x1, Pallas kernels: 48.8 us -> 44.4 us  [body(): pl.pallas_call(functools.partial(unroll_kernel, s), grid_spec=pltpu.Prefe...]
    unnamed x6 -> x22, local copies, waits for them, and re-layouts: 0.84 us -> 3.11 us
  transfers between devices with their start and end apart: 18 -> 18, of which waited for: 11 -> 11; matrix products, arithmetic and copies ran while one was open for 1% -> 2% of each run, Pallas kernels for 7% -> 7%
where the time goes in v2:
time: 107 us
  Pallas kernels  54.6 us (51%)
  waiting for transfers between devices  34.8 us (33%)
  starting transfers between devices  11.9 us (11%)
  local copies, waits for them, and re-layouts  3.79 us (4%)
  other arithmetic  1.36 us (1%)
    pallas_call x1, Pallas kernels, body(): pl.pallas_call(functools.partial(unroll_kernel, s), grid_spec=pltpu.Prefe...  44.4 us
    ppermute x8, waiting for transfers between devices, swap_within(): return lax.ppermute(value, AXES, pairs)  29.1 us
    ppermute x8, starting transfers between devices, swap_within(): return lax.ppermute(value, AXES, pairs)  7.93 us
    pallas_call x1, Pallas kernels, beside(): pl.pallas_call(functools.partial(logits_kernel, s), grid_spec=pltpu.Prefe...  5.7 us
    ppermute x10, waiting for transfers between devices, swap(): return lax.ppermute(value, axis, pairs)  5.69 us
    ppermute x10, starting transfers between devices, swap(): return lax.ppermute(value, axis, pairs)  3.92 us
    unnamed x22, local copies, waits for them, and re-layouts  3.11 us
  transfers between devices with their start and end apart: 18, of which 11 were waited for; matrix products, arithmetic and copies ran while one was open for 2% of the time, Pallas kernels for 7%

profile of v2, /device:TPU:9, one launch (start us, length us, event | category | flops | bytes accessed | tf_op | source)
XLA Modules:
  0.0 107.1 jit_solution(1875465264536086212)
XLA Ops:
  0.6 0.7 collective-permute-start.1
  1.4 0.1 collective-permute-start.2
  1.5 0.4 collective-permute-start.3
  1.9 0.1 collective-permute-start
  2.0 0.4 collective-permute-start.4
  2.4 1.6 %collective-permute-done.4.gains_got = bf16[3,256]{1,0:T(4,128)(2,1)S(1)} collective-permute-done((bf16[3,256]{1,0:T(4,128)(2,1)}, bf16[3,256]{1,0:T(4,128)(2,1)S(1)}, u32[]{:S(2)}, u32[]{:S(2)}) %collective-permute-start.4) | collective-permute-done | bytes 1568 | tf_op jit(solution)/shard_map/ppermute | solution.py:649
  4.1 0.0 copy-start.5
  4.1 0.5 copy-done.10
  4.6 0.1 copy-done.8
  4.7 0.1 copy-done.7
  4.8 0.1 copy-done.5
  4.9 0.1 copy-done.6
  5.1 44.4 %unroll.1 = (bf16[10,128,256]{2,1,0:T(8,128)(2,1)}, bf16[10,128,256]{2,1,0:T(8,128)(2,1)}, f32[8,128]{1,0:T(8,128)}, bf16[2560,256]{1,0:T(8,128)(2,1)}, bf16[256...) custom-call(s32[1]{0:T(128)} %bitcast.1.tower_ref, bf16[256,128]{1,0:T(8,128)(2,1)} %root_hbm.1, ...), custom_call_target="tpu_custom_call" | custom-call | flops 5599395840 | bytes 41943040 | tf_op jit(solution)/shard_map/unroll/pallas_call | solution.py:768
  49.4 0.4 collective-permute-start.5
  49.9 2.9 %collective-permute-done.5 = bf16[2560,256]{1,0:T(8,128)(2,1)S(1)} collective-permute-done((bf16[2560,256]{1,0:T(8,128)(2,1)}, bf16[2560,256]{1,0:T(8,128)(2,1)S(1)}, u32[]{:S(2)}, u32[]{:S(2)}) %collective-permute-start.5) | collective-permute-done | bytes 1310752 | tf_op jit(solution)/shard_map/ppermute | solution.py:649
  52.8 1.3 %copy-done = bf16[2560,256]{1,0:T(8,128)(2,1)S(1)} copy-done((bf16[2560,256]{1,0:T(8,128)(2,1)S(1)}, bf16[2560,256]{1,0:T(8,128)(2,1)}, u32[]{:S(2)}) %copy-start) | copy-done | bytes 1310744
  54.1 1.3 %add_and_split.1 = (bf16[640,256]{1,0:T(8,128)(2,1)}, bf16[640,256]{1,0:T(8,128)(2,1)}, bf16[640,256]{1,0:T(8,128)(2,1)}, bf16[640,256]{1,0:T(8,128)(2,1)}) custom-call(s32[1]{0:T(128)} %bitcast.digit_ref, bf16[4,640,256]{2,1,0:T(8,128)(2,1)S(1)} %bitcast.29, bf16[4,640,256]{2,1,0:T(8,128)(2,1)S(1)} %bitcast.30), custom_call_target="tpu_custom_call" | custom-call | tf_op jit(solution)/shard_map/add_and_split/pallas_call | solution.py:703
  55.3 0.4 collective-permute-start.9
  55.7 2.5 %collective-permute-start.7 = (bf16[640,256]{1,0:T(8,128)(2,1)}, bf16[640,256]{1,0:T(8,128)(2,1)S(1)}, u32[]{:S(2)}, u32[]{:S(2)}) collective-permute-start(bf16[640,256]{1,0:T(8,128)(2,1)} %get-tuple-element.63), channel_id=1, source_target_pairs={{0,2},{1,3},{2,0},{3,1},{4,6},{5,7},{6,4},{7,5},{8,10},{9,11},{10,... | collective-permute-start | bytes 983048 | tf_op jit(solution)/shard_map/ppermute | solution.py:674
  58.2 0.2 collective-permute-start.8
  58.4 0.7 slice_bitcast_fusion
  59.0 1.0 collective-permute-start.10
  60.0 0.8 collective-permute-done.10
  60.8 0.3 collective-permute-start.11
  61.1 0.6 maximum_select_fusion.1
  61.7 0.3 collective-permute-done.11
  62.0 0.7 fusion.2
  62.7 0.8 copy-done.4
  63.6 5.7 %latents_and_logits.1 = (bf16[10,256,256]{2,1,0:T(8,128)(2,1)}, bf16[10,601,256]{2,1,0:T(8,128)(2,1)}) custom-call(s32[1]{0:T(128)} %bitcast.1.tower_ref, bf16[10,128,256]{2,1,0:T(8,128)(2,1)} %get-tuple-element.65.lat_own, bf16[10,128,256]{2,1,0:T(8,128)(2,1)} %copy-done.4, bf16[601,256]{1,0:T(8,128)(2,1)} %bitcast.42), custom_call_target="tpu_custom_call" | custom-call | flops 796917760 | bytes 6291456 | tf_op jit(solution)/shard_map/latents_and_logits/pallas_call | solution.py:867
  69.3 0.3 collective-permute-done.7.refs_2_
  69.6 4.3 %collective-permute-done.8.refs_3_ = bf16[640,256]{1,0:T(8,128)(2,1)S(1)} collective-permute-done((bf16[640,256]{1,0:T(8,128)(2,1)}, bf16[640,256]{1,0:T(8,128)(2,1)S(1)}, u32[]{:S(2)}, u32[]{:S(2)}) %collective-permute-start.8) | collective-permute-done | bytes 327712 | tf_op jit(solution)/shard_map/ppermute | solution.py:674
  73.9 0.2 add_up.3.refs_0_
  74.1 1.3 %collective-permute-start.12 = (bf16[640,256]{1,0:T(8,128)(2,1)S(1)}, bf16[640,256]{1,0:T(8,128)(2,1)S(1)}, u32[]{:S(2)}, u32[]{:S(2)}) collective-permute-start(bf16[640,256]{1,0:T(8,128)(2,1)S(1)} %add_up.3.refs_0_), channel_id=1, source_target_pairs={{0,4},{1,5},{2,6},{3,7},{4,0},{5,1},{6,2},{7,3},{8,12},{9,13},{10,... | collective-permute-start | bytes 983048 | tf_op jit(solution)/shard_map/ppermute | solution.py:674
  75.4 4.7 %collective-permute-done.12.refs_1_ = bf16[640,256]{1,0:T(8,128)(2,1)S(1)} collective-permute-done((bf16[640,256]{1,0:T(8,128)(2,1)S(1)}, bf16[640,256]{1,0:T(8,128)(2,1)S(1)}, u32[]{:S(2)}, u32[]{:S(2)}) %collective-permute-start.12) | collective-permute-done | bytes 327712 | tf_op jit(solution)/shard_map/ppermute | solution.py:674
  80.1 0.1 add_up.4.refs_0_
  80.2 1.3 %collective-permute-start.13 = (bf16[640,256]{1,0:T(8,128)(2,1)S(1)}, bf16[640,256]{1,0:T(8,128)(2,1)S(1)}, u32[]{:S(2)}, u32[]{:S(2)}) collective-permute-start(bf16[640,256]{1,0:T(8,128)(2,1)S(1)} %add_up.4.refs_0_), channel_id=1, source_target_pairs={{0,8},{1,9},{2,10},{3,11},{4,12},{5,13},{6,14},{7,15},{8,0},{9,1},... | collective-permute-start | bytes 983048 | tf_op jit(solution)/shard_map/ppermute | solution.py:674
  81.5 4.7 %collective-permute-done.13.refs_1_ = bf16[640,256]{1,0:T(8,128)(2,1)S(1)} collective-permute-done((bf16[640,256]{1,0:T(8,128)(2,1)S(1)}, bf16[640,256]{1,0:T(8,128)(2,1)S(1)}, u32[]{:S(2)}, u32[]{:S(2)}) %collective-permute-start.13) | collective-permute-done | bytes 327712 | tf_op jit(solution)/shard_map/ppermute | solution.py:674
  86.1 0.1 add_up.5.refs_0_
  86.2 0.1 collective-permute-start.14
  86.3 2.5 %collective-permute-start.15 = (bf16[640,256]{1,0:T(8,128)(2,1)S(1)}, bf16[640,256]{1,0:T(8,128)(2,1)S(1)}, u32[]{:S(2)}, u32[]{:S(2)}) collective-permute-start(bf16[640,256]{1,0:T(8,128)(2,1)S(1)} %add_up.5.refs_0_), channel_id=1, source_target_pairs={{0,2},{1,3},{2,0},{3,1},{4,6},{5,7},{6,4},{7,5},{8,10},{9,11},{10,... | collective-permute-start | bytes 983048 | tf_op jit(solution)/shard_map/ppermute | solution.py:674
  88.8 0.2 collective-permute-start.16
  88.9 4.8 %collective-permute-done.14.refs_1_ = bf16[640,256]{1,0:T(8,128)(2,1)S(1)} collective-permute-done((bf16[640,256]{1,0:T(8,128)(2,1)S(1)}, bf16[640,256]{1,0:T(8,128)(2,1)S(1)}, u32[]{:S(2)}, u32[]{:S(2)}) %collective-permute-start.14) | collective-permute-done | bytes 327712 | tf_op jit(solution)/shard_map/ppermute | solution.py:674
  93.7 6.1 %collective-permute-done.15.refs_2_ = bf16[640,256]{1,0:T(8,128)(2,1)S(1)} collective-permute-done((bf16[640,256]{1,0:T(8,128)(2,1)S(1)}, bf16[640,256]{1,0:T(8,128)(2,1)S(1)}, u32[]{:S(2)}, u32[]{:S(2)}) %collective-permute-start.15) | collective-permute-done | bytes 327712 | tf_op jit(solution)/shard_map/ppermute | solution.py:674
  99.9 4.1 %collective-permute-done.16.refs_3_ = bf16[640,256]{1,0:T(8,128)(2,1)S(1)} collective-permute-done((bf16[640,256]{1,0:T(8,128)(2,1)S(1)}, bf16[640,256]{1,0:T(8,128)(2,1)S(1)}, u32[]{:S(2)}, u32[]{:S(2)}) %collective-permute-start.16) | collective-permute-done | bytes 327712 | tf_op jit(solution)/shard_map/ppermute | solution.py:674
  104.0 0.1 collective-permute-start.17
  104.1 0.1 pad_add_fusion.scalars
  104.2 2.0 %unpack_own.1 = (f32[3,256,256]{2,1,0:T(8,128)}, f32[3,256,256]{2,1,0:T(8,128)}, f32[601,1,256]{2,1,0:T(1,128)}, f32[3,1,256]{2,1,0:T(1,128)}, f32[3,2,10]{2,1,0:T(2,128)}) custom-call(s32[2]{0:T(128)S(1)} %pad_add_fusion.scalars, bf16[640,256]{1,0:T(8,128)(2,1)S(1)} %add_up.5.refs_0_, bf16[640,256]{1,0:T(8,128)(2,1)S(1)} %collective-permute-done.14.refs_1_, ...), custom_call_target="tpu_custom_call" | custom-call | tf_op jit(solution)/shard_map/unpack_own/pallas_call | solution.py:915
  106.2 0.9 unpack_shared.1
  (23 shorter events, 0.1 us)
Async XLA Ops:
  0.6 3.4 %collective-permute-start.1 = (bf16[3,256,256]{2,1,0:T(8,128)(2,1)}, bf16[3,256,256]{2,1,0:T(8,128)(2,1)S(1)}, u32[]{:S(2)}, u32[]{:S(2)}) collective-permute-start(bf16[3,256,256]{2,1,0:T(8,128)(2,1)} %bitcast.35), channel_id=1, source_target_pairs={{0,16},{16,0},{1,17},{17,1},{2,18},{18,2},{3,19},{19,3},{4,20},{20... | collective-permute-start | bytes 1179656 | tf_op jit(solution)/shard_map/ppermute | solution.py:649
  1.4 2.7 %collective-permute-start.2 = (bf16[3,256,256]{2,1,0:T(8,128)(2,1)}, bf16[3,256,256]{2,1,0:T(8,128)(2,1)S(1)}, u32[]{:S(2)}, u32[]{:S(2)}) collective-permute-start(bf16[3,256,256]{2,1,0:T(8,128)(2,1)} %bitcast.37), channel_id=1, source_target_pairs={{0,16},{16,0},{1,17},{17,1},{2,18},{18,2},{3,19},{19,3},{4,20},{20... | collective-permute-start | bytes 1179656 | tf_op jit(solution)/shard_map/ppermute | solution.py:649
  1.5 2.6 %collective-permute-start.3 = (bf16[601,256]{1,0:T(8,128)(2,1)}, bf16[601,256]{1,0:T(8,128)(2,1)S(1)}, u32[]{:S(2)}, u32[]{:S(2)}) collective-permute-start(bf16[601,256]{1,0:T(8,128)(2,1)} %bitcast.40), channel_id=1, source_target_pairs={{0,16},{16,0},{1,17},{17,1},{2,18},{18,2},{3,19},{19,3},{4,20},{20... | collective-permute-start | bytes 923144 | tf_op jit(solution)/shard_map/ppermute | solution.py:649
  1.9 2.2 %collective-permute-start = (bf16[256,128]{1,0:T(8,128)(2,1)}, bf16[256,128]{1,0:T(8,128)(2,1)S(1)}, u32[]{:S(2)}, u32[]{:S(2)}) collective-permute-start(bf16[256,128]{1,0:T(8,128)(2,1)} %root_hbm.1), channel_id=1, source_target_pairs={{0,16},{16,0},{1,17},{17,1},{2,18},{18,2},{3,19},{19,3},{4,20},{20... | collective-permute-start | bytes 196616 | tf_op jit(solution)/shard_map/ppermute | solution.py:649
  2.0 2.1 %collective-permute-start.4 = (bf16[3,256]{1,0:T(4,128)(2,1)}, bf16[3,256]{1,0:T(4,128)(2,1)S(1)}, u32[]{:S(2)}, u32[]{:S(2)}) collective-permute-start(bf16[3,256]{1,0:T(4,128)(2,1)} %bitcast.48), channel_id=1, source_target_pairs={{0,16},{16,0},{1,17},{17,1},{2,18},{18,2},{3,19},{19,3},{4,20},{20... | collective-permute-start | bytes 4616 | tf_op jit(solution)/shard_map/ppermute | solution.py:649
  4.1 0.6 copy-start.10
  4.1 0.6 copy-start.8
  4.1 0.7 copy-start.7
  4.1 0.8 copy-start.5
  4.1 0.9 copy-start.6
  49.4 3.3 %collective-permute-start.5 = (bf16[2560,256]{1,0:T(8,128)(2,1)}, bf16[2560,256]{1,0:T(8,128)(2,1)S(1)}, u32[]{:S(2)}, u32[]{:S(2)}) collective-permute-start(bf16[2560,256]{1,0:T(8,128)(2,1)} %get-tuple-element.51), channel_id=1, source_target_pairs={{0,16},{16,0},{1,17},{17,1},{2,18},{18,2},{3,19},{19,3},{4,20},{20... | collective-permute-start | bytes 3932168 | tf_op jit(solution)/shard_map/ppermute | solution.py:649
  52.7 1.3 %copy-start = (bf16[2560,256]{1,0:T(8,128)(2,1)S(1)}, bf16[2560,256]{1,0:T(8,128)(2,1)}, u32[]{:S(2)}) copy-start(bf16[2560,256]{1,0:T(8,128)(2,1)} %get-tuple-element.50) | copy-start | bytes 3932164
  54.1 1.3 %copy-start.3 = (bf16[10,128,256]{2,1,0:T(8,128)(2,1)S(1)}, bf16[10,128,256]{2,1,0:T(8,128)(2,1)}, u32[]{:S(2)}) copy-start(bf16[10,128,256]{2,1,0:T(8,128)(2,1)} %get-tuple-element.66) | copy-start | bytes 1966084
  54.1 6.8 %copy-start.9 = (bf16[128,128]{1,0:T(8,128)(2,1)S(1)}, bf16[128,128]{1,0:T(8,128)(2,1)}, u32[]{:S(2)}) copy-start(bf16[128,128]{1,0:T(8,128)(2,1)} %get-tuple-element.71) | copy-start | bytes 98308
  54.1 8.0 %copy-start.2 = (bf16[128,128]{1,0:T(8,128)(2,1)S(1)}, bf16[128,128]{1,0:T(8,128)(2,1)}, u32[]{:S(2)}) copy-start(bf16[128,128]{1,0:T(8,128)(2,1)} %get-tuple-element.70) | copy-start | bytes 98308
  55.3 7.4 %collective-permute-start.9 = (bf16[10,128,256]{2,1,0:T(8,128)(2,1)S(1)}, bf16[10,128,256]{2,1,0:T(8,128)(2,1)S(1)}, u32[]{:S(2)}, u32[]{:S(2)}) collective-permute-start(bf16[10,128,256]{2,1,0:T(8,128)(2,1)S(1)} %copy-done.3), channel_id=1, source_target_pairs={{0,16},{16,0},{1,17},{17,1},{2,18},{18,2},{3,19},{19,3},{4,20},{20... | collective-permute-start | bytes 1966088 | tf_op jit(solution)/shard_map/ppermute | solution.py:649
  55.7 13.6 %collective-permute-start.6 = (bf16[640,256]{1,0:T(8,128)(2,1)}, bf16[640,256]{1,0:T(8,128)(2,1)S(1)}, u32[]{:S(2)}, u32[]{:S(2)}) collective-permute-start(bf16[640,256]{1,0:T(8,128)(2,1)} %get-tuple-element.62), channel_id=1, source_target_pairs={{0,1},{1,0},{2,3},{3,2},{4,5},{5,4},{6,7},{7,6},{8,9},{9,8},{10,11... | collective-permute-start | bytes 983048 | tf_op jit(solution)/shard_map/ppermute | solution.py:674
  55.7 13.9 %collective-permute-start.7 = (bf16[640,256]{1,0:T(8,128)(2,1)}, bf16[640,256]{1,0:T(8,128)(2,1)S(1)}, u32[]{:S(2)}, u32[]{:S(2)}) collective-permute-start(bf16[640,256]{1,0:T(8,128)(2,1)} %get-tuple-element.63), channel_id=1, source_target_pairs={{0,2},{1,3},{2,0},{3,1},{4,6},{5,7},{6,4},{7,5},{8,10},{9,11},{10,... | collective-permute-start | bytes 983048 | tf_op jit(solution)/shard_map/ppermute | solution.py:674
  58.2 15.7 %collective-permute-start.8 = (bf16[640,256]{1,0:T(8,128)(2,1)}, bf16[640,256]{1,0:T(8,128)(2,1)S(1)}, u32[]{:S(2)}, u32[]{:S(2)}) collective-permute-start(bf16[640,256]{1,0:T(8,128)(2,1)} %get-tuple-element.64), channel_id=1, source_target_pairs={{0,3},{1,2},{2,1},{3,0},{4,7},{5,6},{6,5},{7,4},{8,11},{9,10},{10,... | collective-permute-start | bytes 983048 | tf_op jit(solution)/shard_map/ppermute | solution.py:674
  59.0 1.8 %collective-permute-start.10 = (f32[128]{0:T(128)S(1)}, f32[128]{0:T(128)S(1)}, u32[]{:S(2)}, u32[]{:S(2)}) collective-permute-start(f32[128]{0:T(128)S(1)} %slice_bitcast_fusion), channel_id=1, source_target_pairs={{0,16},{16,0},{1,17},{17,1},{2,18},{18,2},{3,19},{19,3},{4,20},{20... | collective-permute-start | bytes 1544 | tf_op jit(solution)/shard_map/ppermute | solution.py:649
  60.8 1.2 %collective-permute-start.11 = (bf16[128,128]{1,0:T(8,128)(2,1)S(1)}, bf16[128,128]{1,0:T(8,128)(2,1)S(1)}, u32[]{:S(2)}, u32[]{:S(2)}) collective-permute-start(bf16[128,128]{1,0:T(8,128)(2,1)S(1)} %copy-done.9), channel_id=1, source_target_pairs={{0,16},{16,0},{1,17},{17,1},{2,18},{18,2},{3,19},{19,3},{4,20},{20... | collective-permute-start | bytes 98312 | tf_op jit(solution)/shard_map/ppermute | solution.py:649
  62.7 11.2 %copy-start.1 = (bf16[640,256]{1,0:T(8,128)(2,1)S(1)}, bf16[640,256]{1,0:T(8,128)(2,1)}, u32[]{:S(2)}) copy-start(bf16[640,256]{1,0:T(8,128)(2,1)} %get-tuple-element.75.refs_0_) | copy-start | bytes 983044
  62.7 0.8 copy-start.4
  74.1 6.0 %collective-permute-start.12 = (bf16[640,256]{1,0:T(8,128)(2,1)S(1)}, bf16[640,256]{1,0:T(8,128)(2,1)S(1)}, u32[]{:S(2)}, u32[]{:S(2)}) collective-permute-start(bf16[640,256]{1,0:T(8,128)(2,1)S(1)} %add_up.3.refs_0_), channel_id=1, source_target_pairs={{0,4},{1,5},{2,6},{3,7},{4,0},{5,1},{6,2},{7,3},{8,12},{9,13},{10,... | collective-permute-start | bytes 983048 | tf_op jit(solution)/shard_map/ppermute | solution.py:674
  80.2 6.0 %collective-permute-start.13 = (bf16[640,256]{1,0:T(8,128)(2,1)S(1)}, bf16[640,256]{1,0:T(8,128)(2,1)S(1)}, u32[]{:S(2)}, u32[]{:S(2)}) collective-permute-start(bf16[640,256]{1,0:T(8,128)(2,1)S(1)} %add_up.4.refs_0_), channel_id=1, source_target_pairs={{0,8},{1,9},{2,10},{3,11},{4,12},{5,13},{6,14},{7,15},{8,0},{9,1},... | collective-permute-start | bytes 983048 | tf_op jit(solution)/shard_map/ppermute | solution.py:674
  86.2 7.5 %collective-permute-start.14 = (bf16[640,256]{1,0:T(8,128)(2,1)S(1)}, bf16[640,256]{1,0:T(8,128)(2,1)S(1)}, u32[]{:S(2)}, u32[]{:S(2)}) collective-permute-start(bf16[640,256]{1,0:T(8,128)(2,1)S(1)} %add_up.5.refs_0_), channel_id=1, source_target_pairs={{0,1},{1,0},{2,3},{3,2},{4,5},{5,4},{6,7},{7,6},{8,9},{9,8},{10,11... | collective-permute-start | bytes 983048 | tf_op jit(solution)/shard_map/ppermute | solution.py:674
  86.3 13.6 %collective-permute-start.15 = (bf16[640,256]{1,0:T(8,128)(2,1)S(1)}, bf16[640,256]{1,0:T(8,128)(2,1)S(1)}, u32[]{:S(2)}, u32[]{:S(2)}) collective-permute-start(bf16[640,256]{1,0:T(8,128)(2,1)S(1)} %add_up.5.refs_0_), channel_id=1, source_target_pairs={{0,2},{1,3},{2,0},{3,1},{4,6},{5,7},{6,4},{7,5},{8,10},{9,11},{10,... | collective-permute-start | bytes 983048 | tf_op jit(solution)/shard_map/ppermute | solution.py:674
  88.8 15.2 %collective-permute-start.16 = (bf16[640,256]{1,0:T(8,128)(2,1)S(1)}, bf16[640,256]{1,0:T(8,128)(2,1)S(1)}, u32[]{:S(2)}, u32[]{:S(2)}) collective-permute-start(bf16[640,256]{1,0:T(8,128)(2,1)S(1)} %add_up.5.refs_0_), channel_id=1, source_target_pairs={{0,3},{1,2},{2,1},{3,0},{4,7},{5,6},{6,5},{7,4},{8,11},{9,10},{10,... | collective-permute-start | bytes 983048 | tf_op jit(solution)/shard_map/ppermute | solution.py:674
  104.0 2.2 %collective-permute-start.17 = (bf16[400,256]{1,0:T(8,128)(2,1)S(1)}, bf16[400,256]{1,0:T(8,128)(2,1)S(1)}, u32[]{:S(2)}, u32[]{:S(2)}) collective-permute-start(bf16[400,256]{1,0:T(8,128)(2,1)S(1)} %fusion.1.mine), channel_id=1, source_target_pairs={{0,16},{16,0},{1,17},{17,1},{2,18},{18,2},{3,19},{19,3},{4,20},{20... | collective-permute-start | bytes 614408 | tf_op jit(solution)/shard_map/ppermute | solution.py:649
